TPU v7x, 32 devices: a whole 2x2x4 slice. The times are simulated.
32 devices in a mesh: row: 8 (over z, x), loop: 4 (over y, core).
Axes of the slice: x: 2, y: 2, z: 4, core: 2. Of those that a mesh axis runs over, the one named last changes fastest.
Arguments:
- pair: bfloat16 [192, 192, 128], P('row', 'loop'), may hold values from -6 to 6
- ln_in_gain: float32 [128], replicated, may hold values from 0.1 to 1.9
- ln_in_bias: float32 [128], replicated, may hold values from -3 to 3
- w_proj: bfloat16 [128, 512], replicated, may hold values from -0.5 to 0.5
- w_gate: bfloat16 [128, 128], replicated, may hold values from -0.5 to 0.5
- ln_out_gain: float32 [128], replicated, may hold values from 0.1 to 1.9
- ln_out_bias: float32 [128], replicated, may hold values from -3 to 3
- w_out: bfloat16 [128, 128], replicated, may hold values from -0.5 to 0.5
Outputs:
- update: bfloat16 [192, 192, 128], P('row', 'loop')
All inputs are finite; a program needn't handle non-finite values.
Results may differ from a plain program's by a relative error of at most 0.0055.
Values may be sent and summed in bfloat16 or wider, within the bound.
No kernel may reach another device: no remote copies, remote signals or barrier semaphores. Data moves between devices by JAX's collectives and lax.ppermute only.
A program may use at most 192 MiB of HBM per device.

v0:
```python
import jax
import jax.numpy as jnp
from jax import lax
from jax.sharding import PartitionSpec as P

epsilon = 1e-05


def layer_norm(values, gain, bias):
    values = values.astype(jnp.float32)
    center = values - jnp.mean(values, axis=-1, keepdims=True)
    spread = jnp.mean(center * center, axis=-1, keepdims=True)
    return center * lax.rsqrt(spread + epsilon) * gain + bias


def gated_pair(flat_normed, weights, hidden):
    projected = jnp.dot(flat_normed, weights, preferred_element_type=jnp.float32)
    return (jax.nn.sigmoid(projected[:, :hidden]) * projected[:, hidden:]).astype(jnp.bfloat16)


def on_device(pair, ln_in_gain, ln_in_bias, w_proj, w_gate, ln_out_gain, ln_out_bias, w_out):
    local_rows, local_cols, channels = pair.shape
    hidden = w_out.shape[0]
    normed = layer_norm(pair, ln_in_gain, ln_in_bias).astype(jnp.bfloat16)
    flat_normed = normed.reshape(local_rows * local_cols, channels)
    left = gated_pair(flat_normed, w_proj[:, : 2 * hidden], hidden).reshape(
        local_rows, local_cols, hidden
    )
    right = gated_pair(flat_normed, w_proj[:, 2 * hidden :], hidden).reshape(
        local_rows, local_cols, hidden
    )
    left_wide = lax.all_gather(left, "loop", axis=1, tiled=True)
    left_t = lax.all_to_all(left_wide, "row", split_axis=1, concat_axis=0, tiled=True)
    left_major = left_t.transpose(2, 1, 0)
    right_major = right.transpose(2, 0, 1)
    triangle_major = lax.dot_general(
        left_major,
        lax.all_gather(right_major, "row", axis=1, tiled=True),
        (((2,), (1,)), ((0,), (0,))),
        preferred_element_type=jnp.float32,
    )
    triangle = triangle_major.transpose(1, 2, 0)
    mixed = layer_norm(triangle, ln_out_gain, ln_out_bias).astype(jnp.bfloat16)
    outgoing = jnp.dot(
        mixed.reshape(local_rows * local_cols, hidden), w_out, preferred_element_type=jnp.float32
    )
    gating = jax.nn.sigmoid(jnp.dot(flat_normed, w_gate, preferred_element_type=jnp.float32))
    return (gating * outgoing).astype(jnp.bfloat16).reshape(local_rows, local_cols, channels)


def solution(mesh):
    return jax.shard_map(
        on_device,
        mesh=mesh,
        in_specs=(P("row", "loop", None), P(), P(), P(), P(), P(), P(), P()),
        out_specs=P("row", "loop", None),
        check_vma=False,
    )
```

profile of v0, /device:TPU:0, one launch (start us, length us, event | category | flops | bytes accessed | tf_op | source)
XLA Modules:
  0.0 167.8 jit_solution(6140554836699136286)
XLA Ops:
  6.5 0.0 copy-start
  6.5 0.0 all-gather.3.cloned.1.call-start
  6.5 1.2 convert_reduce_fusion
  7.7 1.4 fusion.8
  9.1 1.4 fusion.11
  10.5 0.0 copy-start.2
  10.5 1.2 fusion.22
  11.7 0.2 fusion.16
  11.9 0.8 copy.24
  12.7 0.0 all-gather.3.cloned.1.call-update
  12.7 0.0 all-gather.5.cloned.1.call-start
  12.8 0.3 fusion.20
  13.1 0.2 fusion.12
  13.2 1.3 copy.28
  14.5 0.0 all-gather.5.cloned.1.call-update
  14.5 18.5 %all-gather.3.cloned.1.call-done = bf16[24,192,128]{2,0,1:T(8,128)(2,1)} async-done(((bf16[24,48,128]{2,0,1:T(8,128)(2,1)}), bf16[24,192,128]{2,0,1:T(8,128)(2,1)}) %all-gather.3.cloned.1.call-update) | async-done | bytes 1179664 | tf_op jit(solution)/shard_map/all_gather | solution.py:32
  33.0 5.5 %all-to-all-start = ((bf16[24,192,128]{2,0,1:T(8,128)(2,1)}), bf16[24,192,128]{2,0,1:T(8,128)(2,1)S(1)}, u32[]{:S(2)}, u32[]{:S(2)}) async-start(bf16[24,192,128]{2,0,1:T(8,128)(2,1)} %all-gather.3.cloned.1.call-done), calls=%async_computation | async-start | bytes 2359296 | tf_op jit(solution)/shard_map/all_to_all | solution.py:33
  38.5 0.0 copy-done
  38.5 1.2 fusion.2
  39.7 49.8 %all-to-all-done = bf16[24,192,128]{2,0,1:T(8,128)(2,1)S(1)} async-done(((bf16[24,192,128]{2,0,1:T(8,128)(2,1)}), bf16[24,192,128]{2,0,1:T(8,128)(2,1)S(1)}, u32[]{:S(2)}, u32[]{:S(2)}) %all-to-all-start) | async-done | bytes 1179680 | tf_op jit(solution)/shard_map/all_to_all | solution.py:33
  89.5 0.2 copy.26
  89.7 1.7 %copy.27 = bf16[192,24,128]{0,1,2:T(8,128)(2,1)S(1)} copy(bf16[192,24,128]{2,1,0:T(8,128)(2,1)S(1)} %bitcast.30) | data formatting | bytes 2359296 | tf_op jit(solution)/shard_map/all_to_all | solution.py:33
  91.4 62.4 %all-gather.5.cloned.1.call-done = bf16[128,192,48]{2,1,0:T(8,128)(2,1)} async-done(((bf16[128,24,48]{2,1,0:T(8,128)(2,1)}), bf16[128,192,48]{2,1,0:T(8,128)(2,1)}) %all-gather.5.cloned.1.call-update) | async-done | bytes 2359312 | tf_op jit(solution)/shard_map/all_gather | solution.py:38
  153.8 4.5 %bitcast_reduce_fusion = (f32[24,48]{1,0:T(8,128)S(1)}, f32[128,24,48]{2,1,0:T(8,128)S(1)}) fusion(bf16[128,192,48]{2,1,0:T(8,128)(2,1)} %all-gather.5.cloned.1.call-done, bf16[192,24,128]{0,1,2:T(8,128)(2,1)S(1)} %copy.27), kind=kOutput, calls=%fused_computation.7 | convolution fusion | flops 56769408 | bytes 4133376 | tf_op jit(solution)/shard_map/dot_general | solution.py:36
  158.3 0.0 copy-start.5
  158.3 0.3 multiply_reduce_fusion
  158.6 0.4 copy-done.4
  159.0 0.0 copy-done.5
  159.0 0.3 add_convert_fusion
  159.4 0.5 copy.29
  159.8 0.2 copy-done.1
  160.1 0.9 fusion.3
  (9 shorter events, 0.0 us)
Async XLA Ops:
  6.5 32.0 %copy-start = (bf16[128,128]{1,0:T(8,128)(2,1)S(1)}, bf16[128,128]{1,0:T(8,128)(2,1)}, u32[]{:S(2)}) copy-start(bf16[128,128]{1,0:T(8,128)(2,1)} %param.12) | copy-start | bytes 98308
  6.5 26.5 %all-gather.3.cloned.1.call-start = ((), (), s32[]{:S(2)}) async-start(), calls=%async_computation.1 | async-start | bytes 1474560 | tf_op jit(solution)/shard_map/all_gather | solution.py:32
  10.5 2.2 %copy-start.2 = (bf16[128,512]{1,0:T(8,128)(2,1)S(1)}, bf16[128,512]{1,0:T(8,128)(2,1)}, u32[]{:S(2)}) copy-start(bf16[128,512]{1,0:T(8,128)(2,1)} %param.11) | copy-start | bytes 393220
  12.7 141.1 %all-gather.5.cloned.1.call-start = ((), (), s32[]{:S(2)}) async-start(), calls=%async_computation.2 | async-start | bytes 7077888 | tf_op jit(solution)/shard_map/all_gather | solution.py:38
  33.0 56.5 %all-to-all-start = ((bf16[24,192,128]{2,0,1:T(8,128)(2,1)}), bf16[24,192,128]{2,0,1:T(8,128)(2,1)S(1)}, u32[]{:S(2)}, u32[]{:S(2)}) async-start(bf16[24,192,128]{2,0,1:T(8,128)(2,1)} %all-gather.3.cloned.1.call-done), calls=%async_computation | async-start | bytes 2359296 | tf_op jit(solution)/shard_map/all_to_all | solution.py:33
  158.3 0.7 copy-start.4
  158.3 0.7 copy-start.5
  159.0 1.1 copy-start.1
  159.0 1.1 copy-start.3
Sparse Core Ops, SparseCore 0:
  12.8 20.1 all-gather.2
  35.1 118.6 all-gather.4
where the time goes:
time: 168 us
  waiting for transfers between devices  131 us (78%)
  between operations  13.5 us (8%)
  matrix products  8.13 us (5%)
  starting transfers between devices  5.55 us (3%)
  local copies, waits for them, and re-layouts  5.02 us (3%)
  other arithmetic  4.89 us (3%)
    all_gather x1, waiting for transfers between devices, on_device(): lax.all_gather(right_major, 'row', axis=1, tiled=True)  62.4 us
    all_to_all x1, waiting for transfers between devices, on_device(): lax.all_to_all(left_wide, 'row', split_axis=1, concat_axis=0, tiled=True)  49.8 us
    all_gather x1, waiting for transfers between devices, on_device(): left_wide = lax.all_gather(left, 'loop', axis=1, tiled=True)  18.5 us
    all_to_all x1, starting transfers between devices, on_device(): lax.all_to_all(left_wide, 'row', split_axis=1, concat_axis=0, tiled=True)  5.51 us
    dot_general x1, matrix products, on_device(): lax.dot_general(left_major, lax.all_gather(right_major, 'row', axis=1, ti...  4.54 us
  transfers between devices with their start and end apart: 3, of which 3 were waited for; matrix products, arithmetic and copies ran while one was open for 3% of the time, Pallas kernels for 0%

commit v1 on v0

v1 whole, which is shorter than its diff:
```python
import jax
import jax.numpy as jnp
from jax import lax
from jax.sharding import PartitionSpec as P

epsilon = 1e-05
axes = ("row", "loop")


def on_device(rows, loops, pair, ln_in_gain, ln_in_bias, w_proj, w_gate, ln_out_gain, ln_out_bias, w_out):
    local_rows, local_cols, channels = pair.shape
    hidden = w_out.shape[0]
    devices = rows * loops
    share = hidden // devices
    places = local_rows * local_cols

    values = pair.reshape(places, channels).astype(jnp.float32)
    center = values - jnp.mean(values, axis=-1, keepdims=True)
    spread = jnp.mean(center * center, axis=-1, keepdims=True)
    normed = (center * lax.rsqrt(spread + epsilon) * ln_in_gain + ln_in_bias).astype(jnp.bfloat16)

    weights = w_proj.reshape(channels, 2, 2, devices, share).transpose(2, 3, 1, 4, 0)
    projected = lax.dot_general(
        weights.reshape(4 * hidden, channels),
        normed,
        (((1,), (1,)), ((), ())),
        preferred_element_type=jnp.float32,
    )
    sides = (jax.nn.sigmoid(projected[: 2 * hidden]) * projected[2 * hidden :]).astype(jnp.bfloat16)
    sides = lax.all_to_all(
        sides.reshape(devices, 2 * share, places), axes, split_axis=0, concat_axis=0
    )
    sides = sides.reshape(rows, loops, 2, share, local_rows, local_cols).transpose(2, 3, 0, 4, 1, 5)
    sides = sides.reshape(2, share, rows * local_rows, loops * local_cols)
    triangle = lax.dot_general(
        sides[0], sides[1], (((1,), (1,)), ((0,), (0,))), preferred_element_type=jnp.float32
    ).astype(jnp.bfloat16)
    triangle = triangle.reshape(share, rows, local_rows, loops, local_cols).transpose(1, 3, 0, 2, 4)
    triangle = lax.all_to_all(
        triangle.reshape(devices, share, places), axes, split_axis=0, concat_axis=0
    )
    triangle = triangle.reshape(hidden, places).astype(jnp.float32)
    center = triangle - jnp.mean(triangle, axis=0, keepdims=True)
    spread = jnp.mean(center * center, axis=0, keepdims=True)
    mixed = center * lax.rsqrt(spread + epsilon) * ln_out_gain[:, None] + ln_out_bias[:, None]
    outgoing = lax.dot_general(
        mixed.astype(jnp.bfloat16),
        w_out,
        (((0,), (0,)), ((), ())),
        preferred_element_type=jnp.float32,
    )
    gating = jax.nn.sigmoid(jnp.dot(normed, w_gate, preferred_element_type=jnp.float32))
    return (gating * outgoing).astype(jnp.bfloat16).reshape(local_rows, local_cols, channels)


def solution(mesh):
    rows, loops = mesh.shape["row"], mesh.shape["loop"]
    return jax.shard_map(
        lambda *arrays: on_device(rows, loops, *arrays),
        mesh=mesh,
        in_specs=(P("row", "loop", None), P(), P(), P(), P(), P(), P(), P()),
        out_specs=P("row", "loop", None),
        check_vma=False,
    )
```

time: 168 us -> 52.1 us (0.31)
  waiting for transfers between devices: 131 us -> 27.2 us
  between operations: 13.5 us -> 0.26 us
  matrix products: 8.13 us -> 2.21 us
  starting transfers between devices: 5.55 us -> 10.6 us
    all_gather x2 -> x0, waiting for transfers between devices: 80.9 us -> none  [the longest x1 62.4 us: on_device(): lax.all_gather(right_major, 'row', axis=1, tiled=True)]
    all_to_all x1 -> x2, waiting for transfers between devices: 49.8 us -> 27.2 us  [the longest x1 16.6 us: on_device(): lax.all_to_all(sides.reshape(devices, 2 * share, places), axes, split_axi...]
    dot_general x5 -> x4, matrix products: 8.13 us -> 2.21 us  [the longest x1 1.08 us: on_device(): lax.dot_general(mixed.astype(jnp.bfloat16), w_out, (((0,), (0,)), ((), ()...]
    all_to_all x1 -> x2, starting transfers between devices: 5.51 us -> 10.6 us  [the longest x1 7.3 us: on_device(): lax.all_to_all(sides.reshape(devices, 2 * share, places), axes, split_axi...]
    all_to_all x2 -> x0, local copies, waits for them, and re-layouts: 1.87 us -> none  [on_device(): lax.all_to_all(left_wide, 'row', split_axis=1, concat_axis=0, tiled=True)]
    reshape x2 -> x5, local copies, waits for them, and re-layouts: 2.04 us -> 3.41 us  [the longest x1 1.49 us: on_device(): sides.reshape(rows, loops, 2, share, local_rows, local_cols)]
  transfers between devices with their start and end apart: 3 -> 2, of which waited for: 3 -> 2; matrix products, arithmetic and copies ran while one was open for 3% -> 2% of each run, Pallas kernels for 0% -> 0%
where the time goes in v1:
time: 52.1 us; the launch traced here: 51.8 us
  waiting for transfers between devices  27.2 us (52%)
  starting transfers between devices  10.6 us (20%)
  local copies, waits for them, and re-layouts  6.6 us (13%)
  other arithmetic  4.89 us (9%)
  matrix products  2.21 us (4%)
    all_to_all x1, waiting for transfers between devices, on_device(): lax.all_to_all(sides.reshape(devices, 2 * share, places), axes, split_axi...  16.6 us
    all_to_all x1, waiting for transfers between devices, on_device(): lax.all_to_all(triangle.reshape(devices, share, places), axes, split_axis...  10.7 us
    all_to_all x1, starting transfers between devices, on_device(): lax.all_to_all(sides.reshape(devices, 2 * share, places), axes, split_axi...  7.3 us
    all_to_all x1, starting transfers between devices, on_device(): lax.all_to_all(triangle.reshape(devices, share, places), axes, split_axis...  3.3 us
    reshape x1, local copies, waits for them, and re-layouts, on_device(): sides.reshape(rows, loops, 2, share, local_rows, local_cols)  1.49 us
    reshape x2, local copies, waits for them, and re-layouts, on_device(): triangle.reshape(devices, share, places)  1.4 us
    reduce_sum x1, other arithmetic, on_device(): spread = jnp.mean(center * center, axis=-1, keepdims=True)  1.38 us
    reduce_sum x1, other arithmetic, on_device(): center = values - jnp.mean(values, axis=-1, keepdims=True)  1.25 us
  transfers between devices with their start and end apart: 2, of which 2 were waited for; matrix products, arithmetic and copies ran while one was open for 2% of the time, Pallas kernels for 0%

profile of v1, /device:TPU:0, one launch (start us, length us, event | category | flops | bytes accessed | tf_op | source)
XLA Modules:
  0.0 51.8 jit_solution(3245829617529013083)
XLA Ops:
  0.0 0.0 copy-start
  0.0 1.2 %convert_reduce_fusion = f32[24,48]{1,0:T(8,128)S(1)} fusion(bf16[24,48,128]{2,1,0:T(8,128)(2,1)} %param.8), kind=kLoop, calls=%fused_computation.25 | loop fusion | flops 293760 | bytes 299520 | tf_op jit(solution)/shard_map/reduce_sum | solution.py:18
  1.3 1.4 %multiply_reduce_fusion.1 = f32[24,48]{1,0:T(8,128)S(1)} fusion(bf16[24,48,128]{2,1,0:T(8,128)(2,1)} %param.8, f32[24,48]{1,0:T(8,128)S(1)} %broadcast_multiply_fusion), kind=kLoop, calls=%fused_computation.23 | loop fusion | flops 588672 | bytes 304128 | tf_op jit(solution)/shard_map/reduce_sum | solution.py:19
  2.7 1.0 %copy.22 = bf16[128,512]{0,1:T(8,128)(2,1)S(1)} copy(bf16[128,512]{1,0:T(8,128)(2,1)} %param.11) | data formatting | bytes 262144 | tf_op args[3]
  3.8 0.4 add_convert_fusion.1
  4.2 0.5 convolution_bitcast_fusion
  4.6 1.1 %fusion.12 = bf16[32,8,1152]{2,1,0:T(8,128)(2,1)} fusion(f32[512,1152]{1,0:T(8,128)S(1)} %convolution_bitcast_fusion), kind=kLoop, calls=%fused_computation.24 | loop fusion | flops 1474560 | bytes 2949120 | tf_op jit(solution)/shard_map/reshape | solution.py:31
  5.8 7.3 %all-to-all-start = ((bf16[32,8,1152]{2,1,0:T(8,128)(2,1)}), bf16[32,8,1152]{2,1,0:T(8,128)(2,1)S(1)}, u32[]{:S(2)}, u32[]{:S(2)}) async-start(bf16[32,8,1152]{2,1,0:T(8,128)(2,1)} %fusion.12), calls=%async_computation | async-start | bytes 1179648 | tf_op jit(solution)/shard_map/all_to_all | solution.py:30
  13.1 0.1 rsqrt.21
  13.2 0.1 div.21
  13.2 16.6 %all-to-all-done = bf16[32,8,1152]{2,1,0:T(8,128)(2,1)S(1)} async-done(((bf16[32,8,1152]{2,1,0:T(8,128)(2,1)}), bf16[32,8,1152]{2,1,0:T(8,128)(2,1)S(1)}, u32[]{:S(2)}, u32[]{:S(2)}) %all-to-all-start) | async-done | bytes 589856 | tf_op jit(solution)/shard_map/all_to_all | solution.py:30
  29.8 1.5 %reshape.107 = bf16[8,4,2,4,24,48]{5,4,3,2,1,0:T(8,128)(2,1)S(1)} reshape(bf16[32,8,1152]{2,1,0:T(8,128)(2,1)S(1)} %all-to-all-done) | data formatting | bytes 1179648 | tf_op jit(solution)/shard_map/reshape | solution.py:33
  31.3 0.3 fusion.17
  31.6 0.4 copy.24
  32.0 0.4 squeeze.6
  32.4 0.4 copy.25
  32.8 0.4 squeeze.7
  33.2 0.4 convolution_convert_fusion
  33.6 0.4 reshape.108
  34.0 0.1 copy.31
  34.2 0.5 %reshape.109 = bf16[32,4,1152]{2,0,1:T(8,128)(2,1)S(1)} reshape(bf16[8,4,4,24,48]{4,3,1,0,2:T(8,128)(2,1)S(1)} %bitcast.36) | data formatting | bytes 589824 | tf_op jit(solution)/shard_map/reshape | solution.py:40
  34.7 0.9 %copy.28 = bf16[32,4,1152]{2,1,0:T(4,128)(2,1)} copy(bf16[32,4,1152]{2,0,1:T(8,128)(2,1)S(1)} %reshape.109) | data formatting | bytes 589824 | tf_op jit(solution)/shard_map/reshape | solution.py:40
  35.6 3.3 %all-to-all-start.1 = ((bf16[32,4,1152]{2,1,0:T(4,128)(2,1)}), bf16[32,4,1152]{2,1,0:T(4,128)(2,1)S(1)}, u32[]{:S(2)}, u32[]{:S(2)}) async-start(bf16[32,4,1152]{2,1,0:T(4,128)(2,1)} %copy.28), calls=%async_computation.1 | async-start | bytes 589824 | tf_op jit(solution)/shard_map/all_to_all | solution.py:39
  38.9 0.4 fusion.11
  39.3 0.3 fusion.2
  39.6 0.0 copy-start.2
  39.6 0.0 copy-start.5
  39.6 0.0 copy-start.6
  39.6 10.7 %all-to-all-done.1 = bf16[32,4,1152]{2,1,0:T(4,128)(2,1)S(1)} async-done(((bf16[32,4,1152]{2,1,0:T(4,128)(2,1)}), bf16[32,4,1152]{2,1,0:T(4,128)(2,1)S(1)}, u32[]{:S(2)}, u32[]{:S(2)}) %all-to-all-start.1) | async-done | bytes 294944 | tf_op jit(solution)/shard_map/all_to_all | solution.py:39
  50.3 0.1 convert_reduce_fusion.1
  50.4 0.2 multiply_reduce_fusion
  50.7 1.1 %fusion.3 = bf16[1152,128]{1,0:T(8,128)(2,1)} fusion(f32[1152,128]{1,0:T(8,128)S(1)} %fusion.2, bf16[128,128]{1,0:T(8,128)(2,1)S(1)} %copy-done.2, f32[128,1152]{1,0:T(8,128)S(1)} %reshape.112, f32[128]{0:T(128)S(1)} %copy-done.5, f32[128]{0:T(128)S(1)} %copy-done.6, f32[1152]{0:T(1024)S(1)} %add_rsqrt_fusion.1, f32[1152]{0:T(1024)S(1)} %broadcast_multiply_fusion.1), kind=kOutput, calls=%fused_computation.6 | convolution fusion | flops 38780928 | bytes 1517568 | tf_op jit(solution)/shard_map/dot_general | solution.py:46
  (16 shorter events, 0.1 us)
Async XLA Ops:
  0.0 39.2 %copy-start = (bf16[128,128]{1,0:T(8,128)(2,1)S(1)}, bf16[128,128]{1,0:T(8,128)(2,1)}, u32[]{:S(2)}) copy-start(bf16[128,128]{1,0:T(8,128)(2,1)} %param.12) | copy-start | bytes 98308
  0.0 3.8 %copy-start.1 = (bf16[24,48,128]{2,1,0:T(8,128)(2,1)S(1)}, bf16[24,48,128]{2,1,0:T(8,128)(2,1)}, u32[]{:S(2)}) copy-start(bf16[24,48,128]{2,1,0:T(8,128)(2,1)} %param.8) | copy-start | bytes 884740
  0.0 3.8 %copy-start.3 = (f32[128]{0:T(128)S(1)}, f32[128]{0:T(128)}, u32[]{:S(2)}) copy-start(f32[128]{0:T(128)} %param.10) | copy-start | bytes 1540
  0.0 3.8 %copy-start.4 = (f32[128]{0:T(128)S(1)}, f32[128]{0:T(128)}, u32[]{:S(2)}) copy-start(f32[128]{0:T(128)} %param.9) | copy-start | bytes 1540
  5.8 24.0 %all-to-all-start = ((bf16[32,8,1152]{2,1,0:T(8,128)(2,1)}), bf16[32,8,1152]{2,1,0:T(8,128)(2,1)S(1)}, u32[]{:S(2)}, u32[]{:S(2)}) async-start(bf16[32,8,1152]{2,1,0:T(8,128)(2,1)} %fusion.12), calls=%async_computation | async-start | bytes 1179648 | tf_op jit(solution)/shard_map/all_to_all | solution.py:30
  35.6 14.7 %all-to-all-start.1 = ((bf16[32,4,1152]{2,1,0:T(4,128)(2,1)}), bf16[32,4,1152]{2,1,0:T(4,128)(2,1)S(1)}, u32[]{:S(2)}, u32[]{:S(2)}) async-start(bf16[32,4,1152]{2,1,0:T(4,128)(2,1)} %copy.28), calls=%async_computation.1 | async-start | bytes 589824 | tf_op jit(solution)/shard_map/all_to_all | solution.py:39
  39.6 11.1 %copy-start.2 = (bf16[128,128]{1,0:T(8,128)(2,1)S(1)}, bf16[128,128]{1,0:T(8,128)(2,1)}, u32[]{:S(2)}) copy-start(bf16[128,128]{1,0:T(8,128)(2,1)} %param.15) | copy-start | bytes 98308
  39.6 11.1 %copy-start.5 = (f32[128]{0:T(128)S(1)}, f32[128]{0:T(128)}, u32[]{:S(2)}) copy-start(f32[128]{0:T(128)} %param.14) | copy-start | bytes 1540
  39.6 11.1 %copy-start.6 = (f32[128]{0:T(128)S(1)}, f32[128]{0:T(128)}, u32[]{:S(2)}) copy-start(f32[128]{0:T(128)} %param.13) | copy-start | bytes 1540

commit v2 on v1

v2 whole, which is shorter than its diff:
```python
import functools

import jax
import jax.numpy as jnp
from jax import lax
from jax.experimental import pallas as pl
from jax.experimental.pallas import tpu as pltpu
from jax.sharding import PartitionSpec as P

epsilon = 1e-05
axes = ("row", "loop")
in_vmem = pl.BlockSpec(memory_space=pltpu.VMEM)
in_hbm = pl.BlockSpec(memory_space=pltpu.HBM)
vmem_bytes = 48 * 2**20
all_vmem_bytes = 66 * 10**6


def sides_kernel(chunk, devices, pair_any, gain_any, bias_any, w_any, out_ref, pair_ref, gain_ref, bias_ref, w_ref, sems):
    places = pair_ref.shape[0]
    wide = w_ref.shape[1]
    half, hidden = wide // 2, wide // 4
    share = hidden // devices
    starts = list(range(0, places, chunk))
    copies = [
        pltpu.make_async_copy(w_any, w_ref, sems.at[0]),
        pltpu.make_async_copy(gain_any, gain_ref, sems.at[1]),
        pltpu.make_async_copy(bias_any, bias_ref, sems.at[2]),
    ]
    for n, first in enumerate(starts):
        part = pl.ds(first, chunk)
        copies.append(pltpu.make_async_copy(pair_any.at[part], pair_ref.at[part], sems.at[3 + n]))
    for copy in copies:
        copy.start()

    row = lax.broadcasted_iota(jnp.int32, (1, wide), 1)
    value, row = row // half, row % half
    owner, row = row // (2 * share), row % (2 * share)
    column = ((row // share) * 2 + value) * hidden + owner * share + row % share
    source = lax.broadcasted_iota(jnp.int32, (wide, wide), 0)
    pick = jnp.where(source == column, 1.0, 0.0).astype(jnp.bfloat16)
    copies[0].wait()
    weights = jnp.dot(w_ref[...], pick, preferred_element_type=jnp.float32)
    weights = weights.T.astype(jnp.bfloat16)
    copies[1].wait()
    copies[2].wait()
    for n, first in enumerate(starts):
        copies[3 + n].wait()
        values = pair_ref[first : first + chunk, :].astype(jnp.float32)
        center = values - jnp.mean(values, axis=-1, keepdims=True)
        spread = jnp.mean(center * center, axis=-1, keepdims=True)
        normed = center * lax.rsqrt(spread + epsilon) * gain_ref[...] + bias_ref[...]
        projected = lax.dot_general(
            weights,
            normed.astype(jnp.bfloat16),
            (((1,), (1,)), ((), ())),
            preferred_element_type=jnp.float32,
        )
        sides = jax.nn.sigmoid(projected[:half]) * projected[half:]
        out_ref[:, first : first + chunk] = sides.astype(jnp.bfloat16)


def triangle_kernel(rows, loops, local_rows, local_cols, pad, in_ref, out_ref, sides_ref, tri_ref):
    both = in_ref.shape[1]
    share = both // 2
    tokens = rows * local_rows
    tiles = loops * pad // 128
    blank = jnp.zeros((both, pad - local_cols), jnp.float32)

    @pl.loop(0, rows)
    def unpack(r):
        blocks = [in_ref[r * loops + l].astype(jnp.float32) for l in range(loops)]
        for k in range(local_rows):
            line = []
            for block in blocks:
                line.append(block[:, k * local_cols : (k + 1) * local_cols])
                if pad > local_cols:
                    line.append(blank)
            line = jnp.concatenate(line, axis=1)
            for t in range(tiles):
                place = pl.ds(t * both * tokens + r * local_rows + k, both, stride=tokens)
                sides_ref[place, :] = line[:, t * 128 : (t + 1) * 128]

    def matrix(index):
        return jnp.concatenate(
            [sides_ref[pl.ds((t * both + index) * tokens, tokens), :] for t in range(tiles)], axis=1
        ).astype(jnp.bfloat16)

    for c in range(share):
        product = lax.dot_general(
            matrix(c), matrix(share + c), (((0,), (0,)), ((), ())), preferred_element_type=jnp.float32
        )
        for t in range(tiles):
            tri_ref[pl.ds((t * share + c) * loops * pad, loops * pad), :] = product[:, t * 128 : (t + 1) * 128]

    @pl.loop(0, rows)
    def pack(r):
        begin = r * local_rows
        begin = (begin // local_cols) * pad + begin % local_cols
        for l in range(loops):
            first, last = l * pad // 128, -(-(l * pad + local_cols) // 128)
            line = []
            for k in range(local_rows):
                here = [
                    tri_ref[pl.ds(t * share * loops * pad + begin + k, share, stride=loops * pad), :]
                    for t in range(first, last)
                ]
                offset = l * pad - first * 128
                line.append(jnp.concatenate(here, axis=1)[:, offset : offset + local_cols])
            out_ref[r * loops + l] = jnp.concatenate(line, axis=1).astype(jnp.bfloat16)


def line_triangle_kernel(rows, loops, local_rows, local_cols, in_ref, out_ref, sides_ref, tri_ref):
    both = in_ref.shape[1]
    share = both // 2
    places = local_rows * local_cols
    tokens = rows * local_rows
    pairs = loops // 2
    group = local_cols // local_rows
    lane = lax.broadcasted_iota(jnp.int32, (both, 128), 1)

    @pl.loop(0, rows, unroll=4 if rows % 4 == 0 else 1)
    def unpack(r):
        for pair in range(pairs):
            one = in_ref[r * loops + 2 * pair].astype(jnp.float32)
            two = in_ref[r * loops + 2 * pair + 1].astype(jnp.float32)
            one = [one[:, u * 128 : (u + 1) * 128] for u in range(places // 128)]
            two = [pltpu.roll(two[:, u * 128 : (u + 1) * 128], 64, 1) for u in range(places // 128)]
            for k in range(local_rows):
                u, offset = divmod(k * local_cols, 128)
                a, b = one[u], two[u]
                if offset + local_cols > 128:
                    a = jnp.where(lane >= offset, a, one[u + 1])
                    b = jnp.where(lane < 64, b, two[u + 1])
                if offset <= 64:
                    is_a = (lane >= offset) & (lane < offset + 64)
                else:
                    is_a = (lane >= offset) | (lane < offset - 64)
                line = pltpu.roll(jnp.where(is_a, a, b), (128 - offset) % 128, 1)
                sides_ref[pl.ds(pair * both * tokens + r * local_rows + k, both, stride=tokens), :] = line

    def matrix(index):
        return jnp.concatenate(
            [sides_ref[pl.ds((t * both + index) * tokens, tokens), :] for t in range(pairs)], axis=1
        ).astype(jnp.bfloat16)

    for c in range(share):
        product = lax.dot_general(
            matrix(c), matrix(share + c), (((0,), (0,)), ((), ())), preferred_element_type=jnp.float32
        )
        for t in range(pairs):
            for l in range(loops):
                for h in range(group):
                    place = (((t * group + h) * share + c) * loops + l) * local_rows
                    first = l * 64 + h * local_rows
                    tri_ref[place : place + local_rows, :] = product[
                        first : first + local_rows, t * 128 : (t + 1) * 128
                    ]

    turned = (lane[: group * share] + 64) % 128

    @pl.loop(0, loops, unroll=True)
    def pack(l):
        for t in range(pairs):
            lines = []
            for k in range(local_rows):
                place = t * group * share * loops * local_rows + l * local_rows + k
                line = tri_ref[pl.ds(place, group * share, stride=loops * local_rows), :]
                lines.append(pltpu.roll(line, k * local_cols % 128, 1))
            for side in range(2):
                at = turned if side else lane[: group * share]
                whole = []
                for u in range(places // 128):
                    first, last = u * 128 // local_cols, ((u + 1) * 128 - 1) // local_cols
                    tile = lines[first]
                    for k in range(first + 1, last + 1):
                        tile = jnp.where(at >= k * local_cols - u * 128, lines[k], tile)
                    whole.append(pltpu.roll(tile, 64, 1) if side else tile)
                whole = jnp.concatenate(whole, axis=1)
                for h in range(group):
                    out_ref[(l * group + h) * loops + 2 * t + side] = whole[
                        h * share : (h + 1) * share
                    ].astype(jnp.bfloat16)


def chunk_of(places):
    return next((c for c in (512, 384, 256, 128) if places % c == 0), places)


def make_sides(pair, gain, bias, w_proj, devices):
    places, channels = pair.shape
    wide = w_proj.shape[1]
    chunk = chunk_of(places)
    return pl.pallas_call(
        functools.partial(sides_kernel, chunk, devices),
        out_shape=jax.ShapeDtypeStruct((wide // 2, places), jnp.bfloat16),
        in_specs=[in_hbm] * 4,
        out_specs=in_vmem,
        scratch_shapes=[
            pltpu.VMEM(pair.shape, pair.dtype),
            pltpu.VMEM(gain.shape, gain.dtype),
            pltpu.VMEM(bias.shape, bias.dtype),
            pltpu.VMEM(w_proj.shape, w_proj.dtype),
            pltpu.SemaphoreType.DMA((3 + places // chunk,)),
        ],
        compiler_params=pltpu.CompilerParams(vmem_limit_bytes=all_vmem_bytes),
        name="sides",
    )(pair, gain, bias, w_proj)


def gating_kernel(pair_ref, in_gain_ref, in_bias_ref, w_gate_ref, out_gain_ref, out_bias_ref, w_out_ref, _, gating_ref, columns_ref, w_ref):
    values = pair_ref[...].astype(jnp.float32)
    center = values - jnp.mean(values, axis=-1, keepdims=True)
    spread = jnp.mean(center * center, axis=-1, keepdims=True)
    normed = center * lax.rsqrt(spread + epsilon) * in_gain_ref[...] + in_bias_ref[...]
    gate = jnp.dot(normed.astype(jnp.bfloat16), w_gate_ref[...], preferred_element_type=jnp.float32)
    gating_ref[...] = jax.nn.sigmoid(gate)
    hidden = w_out_ref.shape[0]
    columns_ref[0] = jnp.broadcast_to(out_gain_ref[...], (128, hidden)).T
    columns_ref[1] = jnp.broadcast_to(out_bias_ref[...], (128, hidden)).T
    w_ref[...] = w_out_ref[...]


def make_gating(pair, in_gain, in_bias, w_gate, out_gain, out_bias, w_out, after):
    places, channels = pair.shape
    hidden = w_out.shape[0]
    return pl.pallas_call(
        gating_kernel,
        out_shape=(
            jax.ShapeDtypeStruct((places, channels), jnp.float32),
            jax.ShapeDtypeStruct((2, hidden, 128), jnp.float32),
            jax.ShapeDtypeStruct(w_out.shape, w_out.dtype),
        ),
        in_specs=[in_vmem] * 7 + [in_hbm],
        out_specs=[in_vmem] * 3,
        compiler_params=pltpu.CompilerParams(vmem_limit_bytes=vmem_bytes),
        cost_estimate=pl.CostEstimate(
            flops=2 * places * channels * channels, bytes_accessed=6 * places * channels, transcendentals=places * channels
        ),
        name="gating",
    )(pair, in_gain, in_bias, w_gate, out_gain, out_bias, w_out, after)


def update_kernel(chunk, tri_ref, gating_ref, columns_ref, w_ref, out_any, out_ref, sems):
    places = tri_ref.shape[1]
    copies = []
    for n, first in enumerate(range(0, places, chunk)):
        part = pl.ds(first, chunk)
        values = tri_ref[:, first : first + chunk].astype(jnp.float32)
        center = values - jnp.mean(values, axis=0, keepdims=True)
        spread = jnp.mean(center * center, axis=0, keepdims=True)
        mixed = center * lax.rsqrt(spread + epsilon) * columns_ref[0][:, :1] + columns_ref[1][:, :1]
        outgoing = lax.dot_general(
            mixed.astype(jnp.bfloat16), w_ref[...], (((0,), (0,)), ((), ())), preferred_element_type=jnp.float32
        )
        out_ref[part, :] = (gating_ref[part, :] * outgoing).astype(jnp.bfloat16)
        copies.append(pltpu.make_async_copy(out_ref.at[part], out_any.at[part], sems.at[n]))
        copies[-1].start()
    for copy in copies:
        copy.wait()


def make_update(triangle, gating, columns, w_out):
    places, channels = gating.shape
    chunk = chunk_of(places)
    return pl.pallas_call(
        functools.partial(update_kernel, chunk),
        out_shape=jax.ShapeDtypeStruct((places, channels), jnp.bfloat16),
        in_specs=[in_vmem] * 4,
        out_specs=in_hbm,
        scratch_shapes=[
            pltpu.VMEM((places, channels), jnp.bfloat16),
            pltpu.SemaphoreType.DMA((places // chunk,)),
        ],
        compiler_params=pltpu.CompilerParams(vmem_limit_bytes=vmem_bytes),
        name="update",
    )(triangle, gating, columns, w_out)


def make_triangle(sides, rows, loops, local_rows, local_cols):
    devices, both, places = sides.shape
    share = both // 2
    pad = 64 if local_cols <= 64 else -(-local_cols // 128) * 128
    tokens, tiles = rows * local_rows, loops * pad // 128
    kernel = functools.partial(triangle_kernel, rows, loops, local_rows, local_cols, pad)
    tri_rows = tiles * share * loops * pad
    if (
        local_cols <= 64
        and local_cols % local_rows == 0
        and local_rows % 8 == 0
        and places % 128 == 0
        and loops % 2 == 0
        and both * local_cols <= 16 * local_rows
        and both <= 8
    ):
        kernel = functools.partial(line_triangle_kernel, rows, loops, local_rows, local_cols)
        tri_rows = tiles * share * tokens
    return pl.pallas_call(
        kernel,
        out_shape=jax.ShapeDtypeStruct((devices, share, places), jnp.bfloat16),
        in_specs=[in_vmem],
        out_specs=in_vmem,
        scratch_shapes=[
            pltpu.VMEM((tiles * both * tokens, 128), jnp.float32),
            pltpu.VMEM((tri_rows, 128), jnp.float32),
        ],
        compiler_params=pltpu.CompilerParams(vmem_limit_bytes=vmem_bytes),
        name="triangle",
    )(sides)


def on_device(rows, loops, pair, ln_in_gain, ln_in_bias, w_proj, w_gate, ln_out_gain, ln_out_bias, w_out):
    local_rows, local_cols, channels = pair.shape
    hidden = w_out.shape[0]
    devices = rows * loops
    share = hidden // devices
    places = local_rows * local_cols

    pair = pair.reshape(places, channels)
    in_gain, in_bias = ln_in_gain[None], ln_in_bias[None]
    sides = make_sides(pair, in_gain, in_bias, w_proj, devices)
    sides = lax.all_to_all(
        sides.reshape(devices, 2 * share, places), axes, split_axis=0, concat_axis=0
    )
    triangle = make_triangle(sides, rows, loops, local_rows, local_cols)
    gating, columns, w_out = make_gating(
        pair, in_gain, in_bias, w_gate, ln_out_gain[None], ln_out_bias[None], w_out, triangle
    )
    triangle = lax.all_to_all(triangle, axes, split_axis=0, concat_axis=0)
    update = make_update(triangle.reshape(hidden, places), gating, columns, w_out)
    return update.reshape(local_rows, local_cols, channels)


def solution(mesh):
    rows, loops = mesh.shape["row"], mesh.shape["loop"]
    return jax.shard_map(
        lambda *arrays: on_device(rows, loops, *arrays),
        mesh=mesh,
        in_specs=(P("row", "loop", None), P(), P(), P(), P(), P(), P(), P()),
        out_specs=P("row", "loop", None),
        check_vma=False,
    )
```

time: 52.1 us -> 47.3 us (0.908)
  blocking collectives: 0 us -> 24 us
  waiting for transfers between devices: 27.2 us -> 10.2 us
  Pallas kernels: 0 us -> 8.7 us
  starting transfers between devices: 10.6 us -> 3.3 us
  local copies, waits for them, and re-layouts: 6.6 us -> 0.71 us
  other arithmetic: 4.89 us -> 0 us
  matrix products: 2.21 us -> 0 us
    all_to_all x0 -> x1, blocking collectives: none -> 24 us  [on_device(): lax.all_to_all(sides.reshape(devices, 2 * share, places), axes, split_axi...]
    all_to_all x2 -> x1, waiting for transfers between devices: 27.2 us -> 10.2 us  [on_device(): triangle = lax.all_to_all(triangle, axes, split_axis=0, concat_axis=0)]
    pallas_call x0 -> x4, Pallas kernels: none -> 8.7 us  [the longest x1 3.58 us: make_sides(): pl.pallas_call(functools.partial(sides_kernel, chunk, devices), out_shape...]
    all_to_all x2 -> x1, starting transfers between devices: 10.6 us -> 3.3 us  [on_device(): triangle = lax.all_to_all(triangle, axes, split_axis=0, concat_axis=0)]
    reshape x5 -> x1, local copies, waits for them, and re-layouts: 3.41 us -> 0.07 us  [on_device(): triangle.reshape(hidden, places)]
    reduce_sum x4 -> x0, other arithmetic: 2.98 us -> none  [the longest x1 1.38 us: on_device(): spread = jnp.mean(center * center, axis=-1, keepdims=True)]
    dot_general x4 -> x0, matrix products: 2.21 us -> none  [the longest x1 1.08 us: on_device(): lax.dot_general(mixed.astype(jnp.bfloat16), w_out, (((0,), (0,)), ((), ()...]
    reshape x1 -> x0, other arithmetic: 1.13 us -> none  [on_device(): sides.reshape(devices, 2 * share, places)]
  transfers between devices with their start and end apart: 2 -> 1, of which waited for: 2 -> 1; matrix products, arithmetic and copies ran while one was open for 2% -> 0% of each run, Pallas kernels for 0% -> 1%
where the time goes in v2:
time: 47.3 us; the launch traced here: 47 us
  blocking collectives  24 us (51%)
  waiting for transfers between devices  10.2 us (22%)
  Pallas kernels  8.7 us (18%)
  starting transfers between devices  3.3 us (7%)
  local copies, waits for them, and re-layouts  0.71 us (2%)
    all_to_all x1, blocking collectives, on_device(): lax.all_to_all(sides.reshape(devices, 2 * share, places), axes, split_axi...  24 us
    all_to_all x1, waiting for transfers between devices, on_device(): triangle = lax.all_to_all(triangle, axes, split_axis=0, concat_axis=0)  10.2 us
    pallas_call x1, Pallas kernels, make_sides(): pl.pallas_call(functools.partial(sides_kernel, chunk, devices), out_shape...  3.58 us
    pallas_call x1, Pallas kernels, make_triangle(): pl.pallas_call(kernel, out_shape=jax.ShapeDtypeStruct((devices, share, pl...  3.41 us
    all_to_all x1, starting transfers between devices, on_device(): triangle = lax.all_to_all(triangle, axes, split_axis=0, concat_axis=0)  3.3 us
    pallas_call x1, Pallas kernels, make_update(): pl.pallas_call(functools.partial(update_kernel, chunk), out_shape=jax.Sha...  1.16 us
  transfers between devices with their start and end apart: 1, of which 1 were waited for; matrix products, arithmetic and copies ran while one was open for 0% of the time, Pallas kernels for 1%

profile of v2, /device:TPU:0, one launch (start us, length us, event | category | flops | bytes accessed | tf_op | source)
XLA Modules:
  0.0 47.0 jit_solution(16860650295042099892)
XLA Ops:
  0.0 3.6 %sides.1 = bf16[256,1152]{1,0:T(8,128)(2,1)} custom-call(bf16[1152,128]{1,0:T(8,128)(2,1)} %bitcast.7, f32[1,128]{1,0:T(1,128)} %bitcast.9, f32[1,128]{1,0:T(1,128)} %bitcast.11, bf16[128,512]{1,0:T(8,128)(2,1)} %w_any.1), custom_call_target="tpu_custom_call" | custom-call | tf_op jit(solution)/shard_map/sides/pallas_call | solution.py:193
  3.6 24.0 %all_to_all.10.in_ref = bf16[32,8,1152]{2,1,0:T(8,128)(2,1)S(1)} all-to-all(bf16[32,8,1152]{2,1,0:T(8,128)(2,1)} %bitcast.15), channel_id=1, replica_groups=mesh['row'=8,'loop'=4] {'row','loop'}, dimensions={0} | all-to-all | bytes 1179648 | tf_op jit(solution)/shard_map/all_to_all | solution.py:321
  27.6 3.4 %triangle.1._ = bf16[32,4,1152]{2,1,0:T(4,128)(2,1)} custom-call(bf16[32,8,1152]{2,1,0:T(8,128)(2,1)S(1)} %all_to_all.10.in_ref), custom_call_target="tpu_custom_call" | custom-call | tf_op jit(solution)/shard_map/triangle/pallas_call | solution.py:297
  31.0 0.0 copy-start
  31.0 0.0 copy-start.1
  31.0 0.0 copy-start.2
  31.0 0.0 copy-start.6
  31.1 3.3 %all-to-all-start.1 = ((bf16[32,4,1152]{2,1,0:T(4,128)(2,1)}), bf16[32,4,1152]{2,1,0:T(4,128)(2,1)S(1)}, u32[]{:S(2)}, u32[]{:S(2)}) async-start(bf16[32,4,1152]{2,1,0:T(4,128)(2,1)} %triangle.1._), calls=%async_computation.1 | async-start | bytes 589824 | tf_op jit(solution)/shard_map/all_to_all | solution.py:328
  34.4 0.0 copy-start.3
  34.4 0.0 copy-start.4
  34.4 0.0 copy-start.5
  34.4 0.0 copy-done
  34.4 0.0 copy-done.1
  34.4 0.0 copy-done.2
  34.4 0.0 copy-done.6
  34.4 0.6 %copy-done.3 = f32[128]{0:T(128)S(1)} copy-done((f32[128]{0:T(128)S(1)}, f32[128]{0:T(128)}, u32[]{:S(2)}) %copy-start.3) | copy-done | bytes 536
  35.0 0.0 copy-done.4
  35.0 0.0 copy-done.5
  35.1 0.5 %gating.1 = (f32[1152,128]{1,0:T(8,128)S(1)}, f32[2,128,128]{2,1,0:T(8,128)S(1)}, bf16[128,128]{1,0:T(8,128)(2,1)S(1)}) custom-call(bf16[1152,128]{1,0:T(8,128)(2,1)S(1)} %bitcast.8, f32[1,128]{1,0:T(1,128)S(1)} %bitcast.10, f32[1,128]{1,0:T(1,128)S(1)} %bitcast.12, bf16[128,128]{1,0:T(8,128)(2,1)S(1)} %copy-done.1, f32[1,128]{1,0:T(1,128)S(1)} %bitcast.13, ...), custom_call_target="tpu_custom_call" | custom-call | flops 37748736 | bytes 884736 | tf_op jit(solution)/shard_map/gating/pallas_call | solution.py:226
  35.6 10.2 %all-to-all-done.1 = bf16[32,4,1152]{2,1,0:T(4,128)(2,1)S(1)} async-done(((bf16[32,4,1152]{2,1,0:T(4,128)(2,1)}), bf16[32,4,1152]{2,1,0:T(4,128)(2,1)S(1)}, u32[]{:S(2)}, u32[]{:S(2)}) %all-to-all-start.1) | async-done | bytes 294944 | tf_op jit(solution)/shard_map/all_to_all | solution.py:328
  45.8 0.1 reshape.14.tri_ref
  45.8 1.2 %update.1 = bf16[1152,128]{1,0:T(8,128)(2,1)} custom-call(bf16[128,1152]{1,0:T(8,128)(2,1)S(1)} %reshape.14.tri_ref, f32[1152,128]{1,0:T(8,128)S(1)} %get-tuple-element.8.gating_ref, f32[2,128,128]{2,1,0:T(8,128)S(1)} %get-tuple-element.9.columns_ref, bf16[128,128]{1,0:T(8,128)(2,1)S(1)} %get-tuple-element.10.w_ref), custom_call_target="tpu_custom_call" | custom-call | tf_op jit(solution)/shard_map/update/pallas_call | solution.py:265
Async XLA Ops:
  31.0 3.4 %copy-start = (bf16[24,48,128]{2,1,0:T(8,128)(2,1)S(1)}, bf16[24,48,128]{2,1,0:T(8,128)(2,1)}, u32[]{:S(2)}) copy-start(bf16[24,48,128]{2,1,0:T(8,128)(2,1)} %param.8) | copy-start | bytes 884740
  31.0 3.4 %copy-start.1 = (bf16[128,128]{1,0:T(8,128)(2,1)S(1)}, bf16[128,128]{1,0:T(8,128)(2,1)}, u32[]{:S(2)}) copy-start(bf16[128,128]{1,0:T(8,128)(2,1)} %w_gate_ref.1) | copy-start | bytes 98308
  31.0 3.4 %copy-start.2 = (bf16[128,128]{1,0:T(8,128)(2,1)S(1)}, bf16[128,128]{1,0:T(8,128)(2,1)}, u32[]{:S(2)}) copy-start(bf16[128,128]{1,0:T(8,128)(2,1)} %w_out_ref.1) | copy-start | bytes 98308
  31.0 3.4 %copy-start.6 = (f32[128]{0:T(128)S(1)}, f32[128]{0:T(128)}, u32[]{:S(2)}) copy-start(f32[128]{0:T(128)} %param.14) | copy-start | bytes 1540
  31.1 14.7 %all-to-all-start.1 = ((bf16[32,4,1152]{2,1,0:T(4,128)(2,1)}), bf16[32,4,1152]{2,1,0:T(4,128)(2,1)S(1)}, u32[]{:S(2)}, u32[]{:S(2)}) async-start(bf16[32,4,1152]{2,1,0:T(4,128)(2,1)} %triangle.1._), calls=%async_computation.1 | async-start | bytes 589824 | tf_op jit(solution)/shard_map/all_to_all | solution.py:328
  34.4 0.7 %copy-start.3 = (f32[128]{0:T(128)S(1)}, f32[128]{0:T(128)}, u32[]{:S(2)}) copy-start(f32[128]{0:T(128)} %param.9) | copy-start | bytes 1540
  34.4 0.7 %copy-start.4 = (f32[128]{0:T(128)S(1)}, f32[128]{0:T(128)}, u32[]{:S(2)}) copy-start(f32[128]{0:T(128)} %param.10) | copy-start | bytes 1540
  34.4 0.7 %copy-start.5 = (f32[128]{0:T(128)S(1)}, f32[128]{0:T(128)}, u32[]{:S(2)}) copy-start(f32[128]{0:T(128)} %param.13) | copy-start | bytes 1540

commit v3 on v2

--- a/solution.py
+++ b/solution.py
@@ -109,38 +109,46 @@
             out_ref[r * loops + l] = jnp.concatenate(line, axis=1).astype(jnp.bfloat16)
 
 
-def line_triangle_kernel(rows, loops, local_rows, local_cols, in_ref, out_ref, sides_ref, tri_ref):
+def line_offsets(local_rows, local_cols):
+    return sorted({k * local_cols % 128 for k in range(local_rows)})
+
+
+def line_triangle_kernel(rows, loops, local_rows, local_cols, in_ref, shifts_ref, out_ref, sides_ref, tri_ref):
     both = in_ref.shape[1]
     share = both // 2
     places = local_rows * local_cols
     tokens = rows * local_rows
     pairs = loops // 2
     group = local_cols // local_rows
-    lane = lax.broadcasted_iota(jnp.int32, (both, 128), 1)
-
-    @pl.loop(0, rows, unroll=4 if rows % 4 == 0 else 1)
-    def unpack(r):
+    height = tokens + 8
+    block = loops * local_rows + 8
+    lane = lax.broadcasted_iota(jnp.int32, (rows * both, 128), 1)
+
+    blocks = [jnp.concatenate([in_ref[r * loops + l] for r in range(rows)], axis=0) for l in range(loops)]
+    for n, offset in enumerate(line_offsets(local_rows, local_cols)):
+        stack, target = [], []
         for pair in range(pairs):
-            one = in_ref[r * loops + 2 * pair].astype(jnp.float32)
-            two = in_ref[r * loops + 2 * pair + 1].astype(jnp.float32)
-            one = [one[:, u * 128 : (u + 1) * 128] for u in range(places // 128)]
-            two = [pltpu.roll(two[:, u * 128 : (u + 1) * 128], 64, 1) for u in range(places // 128)]
             for k in range(local_rows):
-                u, offset = divmod(k * local_cols, 128)
-                a, b = one[u], two[u]
-                if offset + local_cols > 128:
-                    a = jnp.where(lane >= offset, a, one[u + 1])
-                    b = jnp.where(lane < 64, b, two[u + 1])
-                if offset <= 64:
-                    is_a = (lane >= offset) & (lane < offset + 64)
-                else:
-                    is_a = (lane >= offset) | (lane < offset - 64)
-                line = pltpu.roll(jnp.where(is_a, a, b), (128 - offset) % 128, 1)
-                sides_ref[pl.ds(pair * both * tokens + r * local_rows + k, both, stride=tokens), :] = line
+                u = k * local_cols // 128
+                if k * local_cols % 128 != offset:
+                    continue
+                line = []
+                for side in blocks[2 * pair : 2 * pair + 2]:
+                    tile = side[:, u * 128 : (u + 1) * 128]
+                    if offset + local_cols > 128:
+                        tile = jnp.where(lane >= offset, tile, side[:, (u + 1) * 128 : (u + 2) * 128])
+                    line.append(tile)
+                stack.append(jnp.concatenate(line, axis=1))
+                target.append(pair * both * height + k)
+        lines = jnp.dot(jnp.concatenate(stack, axis=0), shifts_ref[n], preferred_element_type=jnp.float32)
+        for m, place in enumerate(target):
+            for r in range(rows):
+                first = (m * rows + r) * both
+                sides_ref[pl.ds(place + r * local_rows, both, stride=height), :] = lines[first : first + both]
 
     def matrix(index):
         return jnp.concatenate(
-            [sides_ref[pl.ds((t * both + index) * tokens, tokens), :] for t in range(pairs)], axis=1
+            [sides_ref[pl.ds((t * both + index) * height, tokens), :] for t in range(pairs)], axis=1
         ).astype(jnp.bfloat16)
 
     for c in range(share):
@@ -148,26 +156,27 @@
             matrix(c), matrix(share + c), (((0,), (0,)), ((), ())), preferred_element_type=jnp.float32
         )
         for t in range(pairs):
-            for l in range(loops):
-                for h in range(group):
-                    place = (((t * group + h) * share + c) * loops + l) * local_rows
+            for h in range(group):
+                for l in range(loops):
+                    place = ((t * group + h) * share + c) * block + l * local_rows
                     first = l * 64 + h * local_rows
                     tri_ref[place : place + local_rows, :] = product[
                         first : first + local_rows, t * 128 : (t + 1) * 128
                     ]
 
-    turned = (lane[: group * share] + 64) % 128
+    lane = lax.broadcasted_iota(jnp.int32, (group * share, 128), 1)
+    turned = (lane + 64) % 128
 
     @pl.loop(0, loops, unroll=True)
     def pack(l):
         for t in range(pairs):
             lines = []
             for k in range(local_rows):
-                place = t * group * share * loops * local_rows + l * local_rows + k
-                line = tri_ref[pl.ds(place, group * share, stride=loops * local_rows), :]
+                place = t * group * share * block + l * local_rows + k
+                line = tri_ref[pl.ds(place, group * share, stride=block), :]
                 lines.append(pltpu.roll(line, k * local_cols % 128, 1))
             for side in range(2):
-                at = turned if side else lane[: group * share]
+                at = turned if side else lane
                 whole = []
                 for u in range(places // 128):
                     first, last = u * 128 // local_cols, ((u + 1) * 128 - 1) // local_cols
@@ -207,7 +216,7 @@
     )(pair, gain, bias, w_proj)
 
 
-def gating_kernel(pair_ref, in_gain_ref, in_bias_ref, w_gate_ref, out_gain_ref, out_bias_ref, w_out_ref, _, gating_ref, columns_ref, w_ref):
+def prepare_kernel(offsets, local_cols, pair_ref, in_gain_ref, in_bias_ref, w_gate_ref, out_gain_ref, out_bias_ref, w_out_ref, _, gating_ref, columns_ref, w_ref, shifts_ref):
     values = pair_ref[...].astype(jnp.float32)
     center = values - jnp.mean(values, axis=-1, keepdims=True)
     spread = jnp.mean(center * center, axis=-1, keepdims=True)
@@ -218,25 +227,34 @@
     columns_ref[0] = jnp.broadcast_to(out_gain_ref[...], (128, hidden)).T
     columns_ref[1] = jnp.broadcast_to(out_bias_ref[...], (128, hidden)).T
     w_ref[...] = w_out_ref[...]
-
-
-def make_gating(pair, in_gain, in_bias, w_gate, out_gain, out_bias, w_out, after):
+    source = lax.broadcasted_iota(jnp.int32, (256, 128), 0)
+    lane = lax.broadcasted_iota(jnp.int32, (256, 128), 1)
+    for n, offset in enumerate(offsets):
+        wanted = ((lane & 63) + offset) & 127
+        wanted = jnp.where(lane >= 64, wanted + 128, wanted)
+        picked = (source == wanted) & ((lane & 63) < local_cols)
+        shifts_ref[n] = jnp.where(picked, 1.0, 0.0).astype(jnp.bfloat16)
+
+
+def make_prepared(pair, in_gain, in_bias, w_gate, out_gain, out_bias, w_out, after, local_rows, local_cols):
     places, channels = pair.shape
     hidden = w_out.shape[0]
+    offsets = line_offsets(local_rows, local_cols)
     return pl.pallas_call(
-        gating_kernel,
+        functools.partial(prepare_kernel, offsets, local_cols),
         out_shape=(
             jax.ShapeDtypeStruct((places, channels), jnp.float32),
             jax.ShapeDtypeStruct((2, hidden, 128), jnp.float32),
             jax.ShapeDtypeStruct(w_out.shape, w_out.dtype),
+            jax.ShapeDtypeStruct((len(offsets), 256, 128), jnp.bfloat16),
         ),
         in_specs=[in_vmem] * 7 + [in_hbm],
-        out_specs=[in_vmem] * 3,
+        out_specs=[in_vmem] * 4,
         compiler_params=pltpu.CompilerParams(vmem_limit_bytes=vmem_bytes),
         cost_estimate=pl.CostEstimate(
             flops=2 * places * channels * channels, bytes_accessed=6 * places * channels, transcendentals=places * channels
         ),
-        name="gating",
+        name="prepare",
     )(pair, in_gain, in_bias, w_gate, out_gain, out_bias, w_out, after)
 
 
@@ -276,12 +294,14 @@
     )(triangle, gating, columns, w_out)
 
 
-def make_triangle(sides, rows, loops, local_rows, local_cols):
+def make_triangle(sides, shifts, rows, loops, local_rows, local_cols):
     devices, both, places = sides.shape
     share = both // 2
     pad = 64 if local_cols <= 64 else -(-local_cols // 128) * 128
     tokens, tiles = rows * local_rows, loops * pad // 128
+    operands = [sides]
     kernel = functools.partial(triangle_kernel, rows, loops, local_rows, local_cols, pad)
+    sides_rows = tiles * both * tokens
     tri_rows = tiles * share * loops * pad
     if (
         local_cols <= 64
@@ -290,22 +310,24 @@
         and places % 128 == 0
         and loops % 2 == 0
         and both * local_cols <= 16 * local_rows
-        and both <= 8
+        and both == 8
     ):
+        operands.append(shifts)
         kernel = functools.partial(line_triangle_kernel, rows, loops, local_rows, local_cols)
-        tri_rows = tiles * share * tokens
+        sides_rows = tiles * both * (tokens + 8)
+        tri_rows = tiles * share * (local_cols // local_rows) * (loops * local_rows + 8)
     return pl.pallas_call(
         kernel,
         out_shape=jax.ShapeDtypeStruct((devices, share, places), jnp.bfloat16),
-        in_specs=[in_vmem],
+        in_specs=[in_vmem] * len(operands),
         out_specs=in_vmem,
         scratch_shapes=[
-            pltpu.VMEM((tiles * both * tokens, 128), jnp.float32),
+            pltpu.VMEM((sides_rows, 128), jnp.float32),
             pltpu.VMEM((tri_rows, 128), jnp.float32),
         ],
         compiler_params=pltpu.CompilerParams(vmem_limit_bytes=vmem_bytes),
         name="triangle",
-    )(sides)
+    )(*operands)
 
 
 def on_device(rows, loops, pair, ln_in_gain, ln_in_bias, w_proj, w_gate, ln_out_gain, ln_out_bias, w_out):
@@ -318,13 +340,12 @@
     pair = pair.reshape(places, channels)
     in_gain, in_bias = ln_in_gain[None], ln_in_bias[None]
     sides = make_sides(pair, in_gain, in_bias, w_proj, devices)
-    sides = lax.all_to_all(
-        sides.reshape(devices, 2 * share, places), axes, split_axis=0, concat_axis=0
+    sides = sides.reshape(devices, 2 * share, places)
+    gating, columns, w_out, shifts = make_prepared(
+        pair, in_gain, in_bias, w_gate, ln_out_gain[None], ln_out_bias[None], w_out, sides, local_rows, local_cols
     )
-    triangle = make_triangle(sides, rows, loops, local_rows, local_cols)
-    gating, columns, w_out = make_gating(
-        pair, in_gain, in_bias, w_gate, ln_out_gain[None], ln_out_bias[None], w_out, triangle
-    )
+    sides = lax.all_to_all(sides, axes, split_axis=0, concat_axis=0)
+    triangle = make_triangle(sides, shifts, rows, loops, local_rows, local_cols)
     triangle = lax.all_to_all(triangle, axes, split_axis=0, concat_axis=0)
     update = make_update(triangle.reshape(hidden, places), gating, columns, w_out)
     return update.reshape(local_rows, local_cols, channels)

time: 47.3 us -> 44.9 us (0.949)
  blocking collectives: 24 us -> 14.5 us
  waiting for transfers between devices: 10.2 us -> 15.4 us
  starting transfers between devices: 3.3 us -> 7.3 us
  Pallas kernels: 8.7 us -> 6.6 us
    all_to_all x1, blocking collectives: 24 us -> 14.5 us  [on_device(): triangle = lax.all_to_all(triangle, axes, split_axis=0, concat_axis=0)]
    all_to_all x1, waiting for transfers between devices: 10.2 us -> 15.4 us  [on_device(): sides = lax.all_to_all(sides, axes, split_axis=0, concat_axis=0)]
    all_to_all x1, starting transfers between devices: 3.3 us -> 7.3 us  [on_device(): sides = lax.all_to_all(sides, axes, split_axis=0, concat_axis=0)]
    pallas_call x1, Pallas kernels: 3.41 us -> 1.2 us  [make_triangle(): pl.pallas_call(kernel, out_shape=jax.ShapeDtypeStruct((devices, share, pl...]
where the time goes in v3:
time: 44.9 us; the launch traced here: 44.6 us
  waiting for transfers between devices  15.4 us (34%)
  blocking collectives  14.5 us (32%)
  starting transfers between devices  7.3 us (16%)
  Pallas kernels  6.6 us (15%)
  local copies, waits for them, and re-layouts  0.72 us (2%)
    all_to_all x1, waiting for transfers between devices, on_device(): sides = lax.all_to_all(sides, axes, split_axis=0, concat_axis=0)  15.4 us
    all_to_all x1, blocking collectives, on_device(): triangle = lax.all_to_all(triangle, axes, split_axis=0, concat_axis=0)  14.5 us
    all_to_all x1, starting transfers between devices, on_device(): sides = lax.all_to_all(sides, axes, split_axis=0, concat_axis=0)  7.3 us
    pallas_call x1, Pallas kernels, make_sides(): pl.pallas_call(functools.partial(sides_kernel, chunk, devices), out_shape...  3.58 us
    pallas_call x1, Pallas kernels, make_triangle(): pl.pallas_call(kernel, out_shape=jax.ShapeDtypeStruct((devices, share, pl...  1.2 us
    pallas_call x1, Pallas kernels, make_update(): pl.pallas_call(functools.partial(update_kernel, chunk), out_shape=jax.Sha...  1.16 us
  transfers between devices with their start and end apart: 1, of which 1 were waited for; matrix products, arithmetic and copies ran while one was open for 0% of the time, Pallas kernels for 1%

profile of v3, /device:TPU:0, one launch (start us, length us, event | category | flops | bytes accessed | tf_op | source)
XLA Modules:
  0.0 44.6 jit_solution(2453783182260103802)
XLA Ops:
  0.0 3.6 %sides.1 = bf16[256,1152]{1,0:T(8,128)(2,1)} custom-call(bf16[1152,128]{1,0:T(8,128)(2,1)} %bitcast.9, f32[1,128]{1,0:T(1,128)} %bitcast.11, f32[1,128]{1,0:T(1,128)} %bitcast.13, bf16[128,512]{1,0:T(8,128)(2,1)} %w_any.1), custom_call_target="tpu_custom_call" | custom-call | tf_op jit(solution)/shard_map/sides/pallas_call | solution.py:202
  3.6 0.0 copy-start
  3.6 0.0 copy-start.1
  3.6 0.0 copy-start.2
  3.6 0.0 copy-start.3
  3.6 0.0 copy-start.7
  3.6 7.3 %all-to-all-start = ((bf16[32,8,1152]{2,1,0:T(8,128)(2,1)}), bf16[32,8,1152]{2,1,0:T(8,128)(2,1)S(1)}, u32[]{:S(2)}, u32[]{:S(2)}) async-start(bf16[32,8,1152]{2,1,0:T(8,128)(2,1)} %bitcast.7), calls=%async_computation | async-start | bytes 1179648 | tf_op jit(solution)/shard_map/all_to_all | solution.py:347
  11.0 0.0 copy-start.4
  11.0 0.0 copy-start.5
  11.0 0.0 copy-start.6
  11.0 0.0 copy-done
  11.0 0.0 copy-done.1
  11.0 0.0 copy-done.2
  11.0 0.0 copy-done.3
  11.0 0.0 copy-done.7
  11.0 0.6 %copy-done.4 = f32[128]{0:T(128)S(1)} copy-done((f32[128]{0:T(128)S(1)}, f32[128]{0:T(128)}, u32[]{:S(2)}) %copy-start.4) | copy-done | bytes 536
  11.6 0.0 copy-done.5
  11.6 0.0 copy-done.6
  11.6 0.7 %prepare.1 = (f32[1152,128]{1,0:T(8,128)S(1)}, f32[2,128,128]{2,1,0:T(8,128)S(1)}, bf16[128,128]{1,0:T(8,128)(2,1)S(1)}, bf16[8,256,128]{2,1,0:T(8,128)(2,1)S(1)}) custom-call(bf16[1152,128]{1,0:T(8,128)(2,1)S(1)} %bitcast.10, f32[1,128]{1,0:T(1,128)S(1)} %bitcast.12, f32[1,128]{1,0:T(1,128)S(1)} %bitcast.14, bf16[128,128]{1,0:T(8,128)(2,1)S(1)} %copy-done.2, ...), custom_call_target="tpu_custom_call" | custom-call | flops 37748736 | bytes 884736 | tf_op jit(solution)/shard_map/prepare/pallas_call | solution.py:243
  12.3 15.4 %all-to-all-done.in_ref = bf16[32,8,1152]{2,1,0:T(8,128)(2,1)S(1)} async-done(((bf16[32,8,1152]{2,1,0:T(8,128)(2,1)}), bf16[32,8,1152]{2,1,0:T(8,128)(2,1)S(1)}, u32[]{:S(2)}, u32[]{:S(2)}) %all-to-all-start) | async-done | bytes 589856 | tf_op jit(solution)/shard_map/all_to_all | solution.py:347
  27.7 1.2 %triangle.1 = bf16[32,4,1152]{2,1,0:T(4,128)(2,1)S(1)} custom-call(bf16[32,8,1152]{2,1,0:T(8,128)(2,1)S(1)} %all-to-all-done.in_ref, bf16[8,256,128]{2,1,0:T(8,128)(2,1)S(1)} %get-tuple-element.9.shifts_ref), custom_call_target="tpu_custom_call" | custom-call | tf_op jit(solution)/shard_map/triangle/pallas_call | solution.py:319
  28.9 14.5 %all_to_all.10 = bf16[32,4,1152]{2,1,0:T(4,128)(2,1)S(1)} all-to-all(bf16[32,4,1152]{2,1,0:T(4,128)(2,1)S(1)} %triangle.1), channel_id=1, replica_groups=mesh['row'=8,'loop'=4] {'row','loop'}, dimensions={0} | all-to-all | bytes 589824 | tf_op jit(solution)/shard_map/all_to_all | solution.py:349
  43.4 0.1 reshape.14.tri_ref
  43.5 1.2 %update.1 = bf16[1152,128]{1,0:T(8,128)(2,1)} custom-call(bf16[128,1152]{1,0:T(8,128)(2,1)S(1)} %reshape.14.tri_ref, f32[1152,128]{1,0:T(8,128)S(1)} %get-tuple-element.10.gating_ref, f32[2,128,128]{2,1,0:T(8,128)S(1)} %get-tuple-element.11.columns_ref, bf16[128,128]{1,0:T(8,128)(2,1)S(1)} %get-tuple-element.12.w_ref), custom_call_target="tpu_custom_call" | custom-call | tf_op jit(solution)/shard_map/update/pallas_call | solution.py:283
Async XLA Ops:
  3.6 7.4 %copy-start = (bf16[256,1152]{1,0:T(8,128)(2,1)S(1)}, bf16[256,1152]{1,0:T(8,128)(2,1)}, u32[]{:S(2)}) copy-start(bf16[256,1152]{1,0:T(8,128)(2,1)} %sides.1) | copy-start | bytes 1769476
  3.6 7.4 %copy-start.1 = (bf16[24,48,128]{2,1,0:T(8,128)(2,1)S(1)}, bf16[24,48,128]{2,1,0:T(8,128)(2,1)}, u32[]{:S(2)}) copy-start(bf16[24,48,128]{2,1,0:T(8,128)(2,1)} %param.8) | copy-start | bytes 884740
  3.6 7.4 %copy-start.2 = (bf16[128,128]{1,0:T(8,128)(2,1)S(1)}, bf16[128,128]{1,0:T(8,128)(2,1)}, u32[]{:S(2)}) copy-start(bf16[128,128]{1,0:T(8,128)(2,1)} %w_gate_ref.1) | copy-start | bytes 98308
  3.6 7.4 %copy-start.3 = (bf16[128,128]{1,0:T(8,128)(2,1)S(1)}, bf16[128,128]{1,0:T(8,128)(2,1)}, u32[]{:S(2)}) copy-start(bf16[128,128]{1,0:T(8,128)(2,1)} %w_out_ref.1) | copy-start | bytes 98308
  3.6 7.4 %copy-start.7 = (f32[128]{0:T(128)S(1)}, f32[128]{0:T(128)}, u32[]{:S(2)}) copy-start(f32[128]{0:T(128)} %param.14) | copy-start | bytes 1540
  3.6 24.0 %all-to-all-start = ((bf16[32,8,1152]{2,1,0:T(8,128)(2,1)}), bf16[32,8,1152]{2,1,0:T(8,128)(2,1)S(1)}, u32[]{:S(2)}, u32[]{:S(2)}) async-start(bf16[32,8,1152]{2,1,0:T(8,128)(2,1)} %bitcast.7), calls=%async_computation | async-start | bytes 1179648 | tf_op jit(solution)/shard_map/all_to_all | solution.py:347
  11.0 0.7 %copy-start.4 = (f32[128]{0:T(128)S(1)}, f32[128]{0:T(128)}, u32[]{:S(2)}) copy-start(f32[128]{0:T(128)} %param.9) | copy-start | bytes 1540
  11.0 0.7 %copy-start.5 = (f32[128]{0:T(128)S(1)}, f32[128]{0:T(128)}, u32[]{:S(2)}) copy-start(f32[128]{0:T(128)} %param.10) | copy-start | bytes 1540
  11.0 0.7 %copy-start.6 = (f32[128]{0:T(128)S(1)}, f32[128]{0:T(128)}, u32[]{:S(2)}) copy-start(f32[128]{0:T(128)} %param.13) | copy-start | bytes 1540

commit v4 on v3

--- a/solution.py
+++ b/solution.py
@@ -12,25 +12,22 @@
 in_vmem = pl.BlockSpec(memory_space=pltpu.VMEM)
 in_hbm = pl.BlockSpec(memory_space=pltpu.HBM)
 vmem_bytes = 48 * 2**20
-all_vmem_bytes = 66 * 10**6
-
-
-def sides_kernel(chunk, devices, pair_any, gain_any, bias_any, w_any, out_ref, pair_ref, gain_ref, bias_ref, w_ref, sems):
-    places = pair_ref.shape[0]
-    wide = w_ref.shape[1]
+
+
+def line_offsets(local_rows, local_cols):
+    return sorted({k * local_cols % 128 for k in range(local_rows)})
+
+
+def sides_kernel(devices, offsets, local_cols, *refs):
+    given, results, held, sems = refs[:8], refs[8:13], refs[13:21], refs[21]
+    out_ref, gating_ref, columns_ref, w_out_t_ref, shifts_ref = results
+    copies = [pltpu.make_async_copy(*ends, sems.at[n]) for n, ends in enumerate(zip(given, held))]
+    for copy in copies:
+        copy.start()
+    pair_ref, w_proj_ref, w_gate_ref, in_gain_ref, in_bias_ref, out_gain_ref, out_bias_ref, w_out_ref = held
+    wide = w_proj_ref.shape[1]
     half, hidden = wide // 2, wide // 4
     share = hidden // devices
-    starts = list(range(0, places, chunk))
-    copies = [
-        pltpu.make_async_copy(w_any, w_ref, sems.at[0]),
-        pltpu.make_async_copy(gain_any, gain_ref, sems.at[1]),
-        pltpu.make_async_copy(bias_any, bias_ref, sems.at[2]),
-    ]
-    for n, first in enumerate(starts):
-        part = pl.ds(first, chunk)
-        copies.append(pltpu.make_async_copy(pair_any.at[part], pair_ref.at[part], sems.at[3 + n]))
-    for copy in copies:
-        copy.start()
 
     row = lax.broadcasted_iota(jnp.int32, (1, wide), 1)
     value, row = row // half, row % half
@@ -38,25 +35,32 @@
     column = ((row // share) * 2 + value) * hidden + owner * share + row % share
     source = lax.broadcasted_iota(jnp.int32, (wide, wide), 0)
     pick = jnp.where(source == column, 1.0, 0.0).astype(jnp.bfloat16)
-    copies[0].wait()
-    weights = jnp.dot(w_ref[...], pick, preferred_element_type=jnp.float32)
-    weights = weights.T.astype(jnp.bfloat16)
-    copies[1].wait()
-    copies[2].wait()
-    for n, first in enumerate(starts):
-        copies[3 + n].wait()
-        values = pair_ref[first : first + chunk, :].astype(jnp.float32)
-        center = values - jnp.mean(values, axis=-1, keepdims=True)
-        spread = jnp.mean(center * center, axis=-1, keepdims=True)
-        normed = center * lax.rsqrt(spread + epsilon) * gain_ref[...] + bias_ref[...]
-        projected = lax.dot_general(
-            weights,
-            normed.astype(jnp.bfloat16),
-            (((1,), (1,)), ((), ())),
-            preferred_element_type=jnp.float32,
-        )
-        sides = jax.nn.sigmoid(projected[:half]) * projected[half:]
-        out_ref[:, first : first + chunk] = sides.astype(jnp.bfloat16)
+
+    source = lax.broadcasted_iota(jnp.int32, (256, 128), 0)
+    lane = lax.broadcasted_iota(jnp.int32, (256, 128), 1)
+    for n, offset in enumerate(offsets):
+        wanted = ((lane & 63) + offset) & 127
+        wanted = jnp.where(lane >= 64, wanted + 128, wanted)
+        picked = (source == wanted) & ((lane & 63) < local_cols)
+        shifts_ref[n] = jnp.where(picked, 1.0, 0.0).astype(jnp.bfloat16)
+
+    for copy in copies:
+        copy.wait()
+    weights = jnp.dot(w_proj_ref[...], pick, preferred_element_type=jnp.float32).T.astype(jnp.bfloat16)
+    weights = jnp.concatenate([weights, w_gate_ref[...].astype(jnp.float32).T.astype(jnp.bfloat16)], axis=0)
+    values = pair_ref[...].astype(jnp.float32)
+    center = values - jnp.mean(values, axis=-1, keepdims=True)
+    spread = jnp.mean(center * center, axis=-1, keepdims=True)
+    normed = center * lax.rsqrt(spread + epsilon) * in_gain_ref[...] + in_bias_ref[...]
+    projected = lax.dot_general(
+        weights, normed.astype(jnp.bfloat16), (((1,), (1,)), ((), ())), preferred_element_type=jnp.float32
+    )
+    sides = jax.nn.sigmoid(projected[:half]) * projected[half:wide]
+    out_ref[...] = sides.astype(jnp.bfloat16)
+    gating_ref[...] = jax.nn.sigmoid(projected[wide:])
+    columns_ref[0] = jnp.broadcast_to(out_gain_ref[...], (128, hidden)).T
+    columns_ref[1] = jnp.broadcast_to(out_bias_ref[...], (128, hidden)).T
+    w_out_t_ref[...] = w_out_ref[...].astype(jnp.float32).T.astype(jnp.bfloat16)
 
 
 def triangle_kernel(rows, loops, local_rows, local_cols, pad, in_ref, out_ref, sides_ref, tri_ref):
@@ -107,10 +111,6 @@
                 offset = l * pad - first * 128
                 line.append(jnp.concatenate(here, axis=1)[:, offset : offset + local_cols])
             out_ref[r * loops + l] = jnp.concatenate(line, axis=1).astype(jnp.bfloat16)
-
-
-def line_offsets(local_rows, local_cols):
-    return sorted({k * local_cols % 128 for k in range(local_rows)})
 
 
 def line_triangle_kernel(rows, loops, local_rows, local_cols, in_ref, shifts_ref, out_ref, sides_ref, tri_ref):
@@ -191,107 +191,47 @@
                     ].astype(jnp.bfloat16)
 
 
-def chunk_of(places):
-    return next((c for c in (512, 384, 256, 128) if places % c == 0), places)
-
-
-def make_sides(pair, gain, bias, w_proj, devices):
-    places, channels = pair.shape
-    wide = w_proj.shape[1]
-    chunk = chunk_of(places)
-    return pl.pallas_call(
-        functools.partial(sides_kernel, chunk, devices),
-        out_shape=jax.ShapeDtypeStruct((wide // 2, places), jnp.bfloat16),
-        in_specs=[in_hbm] * 4,
-        out_specs=in_vmem,
-        scratch_shapes=[
-            pltpu.VMEM(pair.shape, pair.dtype),
-            pltpu.VMEM(gain.shape, gain.dtype),
-            pltpu.VMEM(bias.shape, bias.dtype),
-            pltpu.VMEM(w_proj.shape, w_proj.dtype),
-            pltpu.SemaphoreType.DMA((3 + places // chunk,)),
-        ],
-        compiler_params=pltpu.CompilerParams(vmem_limit_bytes=all_vmem_bytes),
-        name="sides",
-    )(pair, gain, bias, w_proj)
-
-
-def prepare_kernel(offsets, local_cols, pair_ref, in_gain_ref, in_bias_ref, w_gate_ref, out_gain_ref, out_bias_ref, w_out_ref, _, gating_ref, columns_ref, w_ref, shifts_ref):
-    values = pair_ref[...].astype(jnp.float32)
-    center = values - jnp.mean(values, axis=-1, keepdims=True)
-    spread = jnp.mean(center * center, axis=-1, keepdims=True)
-    normed = center * lax.rsqrt(spread + epsilon) * in_gain_ref[...] + in_bias_ref[...]
-    gate = jnp.dot(normed.astype(jnp.bfloat16), w_gate_ref[...], preferred_element_type=jnp.float32)
-    gating_ref[...] = jax.nn.sigmoid(gate)
-    hidden = w_out_ref.shape[0]
-    columns_ref[0] = jnp.broadcast_to(out_gain_ref[...], (128, hidden)).T
-    columns_ref[1] = jnp.broadcast_to(out_bias_ref[...], (128, hidden)).T
-    w_ref[...] = w_out_ref[...]
-    source = lax.broadcasted_iota(jnp.int32, (256, 128), 0)
-    lane = lax.broadcasted_iota(jnp.int32, (256, 128), 1)
-    for n, offset in enumerate(offsets):
-        wanted = ((lane & 63) + offset) & 127
-        wanted = jnp.where(lane >= 64, wanted + 128, wanted)
-        picked = (source == wanted) & ((lane & 63) < local_cols)
-        shifts_ref[n] = jnp.where(picked, 1.0, 0.0).astype(jnp.bfloat16)
-
-
-def make_prepared(pair, in_gain, in_bias, w_gate, out_gain, out_bias, w_out, after, local_rows, local_cols):
-    places, channels = pair.shape
-    hidden = w_out.shape[0]
+def make_sides(devices, local_rows, local_cols, *given):
+    places, channels = given[0].shape
+    wide = given[1].shape[1]
+    hidden = wide // 4
     offsets = line_offsets(local_rows, local_cols)
     return pl.pallas_call(
-        functools.partial(prepare_kernel, offsets, local_cols),
+        functools.partial(sides_kernel, devices, offsets, local_cols),
         out_shape=(
-            jax.ShapeDtypeStruct((places, channels), jnp.float32),
+            jax.ShapeDtypeStruct((wide // 2, places), jnp.bfloat16),
+            jax.ShapeDtypeStruct((channels, places), jnp.float32),
             jax.ShapeDtypeStruct((2, hidden, 128), jnp.float32),
-            jax.ShapeDtypeStruct(w_out.shape, w_out.dtype),
+            jax.ShapeDtypeStruct((channels, hidden), jnp.bfloat16),
             jax.ShapeDtypeStruct((len(offsets), 256, 128), jnp.bfloat16),
         ),
-        in_specs=[in_vmem] * 7 + [in_hbm],
-        out_specs=[in_vmem] * 4,
+        in_specs=[in_hbm] * len(given),
+        out_specs=[in_vmem] * 5,
+        scratch_shapes=[pltpu.VMEM(x.shape, x.dtype) for x in given] + [pltpu.SemaphoreType.DMA((len(given),))],
         compiler_params=pltpu.CompilerParams(vmem_limit_bytes=vmem_bytes),
-        cost_estimate=pl.CostEstimate(
-            flops=2 * places * channels * channels, bytes_accessed=6 * places * channels, transcendentals=places * channels
-        ),
-        name="prepare",
-    )(pair, in_gain, in_bias, w_gate, out_gain, out_bias, w_out, after)
-
-
-def update_kernel(chunk, tri_ref, gating_ref, columns_ref, w_ref, out_any, out_ref, sems):
-    places = tri_ref.shape[1]
-    copies = []
-    for n, first in enumerate(range(0, places, chunk)):
-        part = pl.ds(first, chunk)
-        values = tri_ref[:, first : first + chunk].astype(jnp.float32)
-        center = values - jnp.mean(values, axis=0, keepdims=True)
-        spread = jnp.mean(center * center, axis=0, keepdims=True)
-        mixed = center * lax.rsqrt(spread + epsilon) * columns_ref[0][:, :1] + columns_ref[1][:, :1]
-        outgoing = lax.dot_general(
-            mixed.astype(jnp.bfloat16), w_ref[...], (((0,), (0,)), ((), ())), preferred_element_type=jnp.float32
-        )
-        out_ref[part, :] = (gating_ref[part, :] * outgoing).astype(jnp.bfloat16)
-        copies.append(pltpu.make_async_copy(out_ref.at[part], out_any.at[part], sems.at[n]))
-        copies[-1].start()
-    for copy in copies:
-        copy.wait()
-
-
-def make_update(triangle, gating, columns, w_out):
-    places, channels = gating.shape
-    chunk = chunk_of(places)
+        name="sides",
+    )(*[pltpu.with_memory_space_constraint(x, pltpu.HBM) for x in given])
+
+
+def update_kernel(tri_ref, gating_ref, columns_ref, w_ref, out_ref):
+    values = tri_ref[...].astype(jnp.float32)
+    center = values - jnp.mean(values, axis=0, keepdims=True)
+    spread = jnp.mean(center * center, axis=0, keepdims=True)
+    mixed = center * lax.rsqrt(spread + epsilon) * columns_ref[0][:, :1] + columns_ref[1][:, :1]
+    outgoing = jnp.dot(w_ref[...], mixed.astype(jnp.bfloat16), preferred_element_type=jnp.float32)
+    out_ref[...] = (gating_ref[...] * outgoing).T.astype(jnp.bfloat16)
+
+
+def make_update(triangle, gating, columns, w_out_t):
+    channels, places = gating.shape
     return pl.pallas_call(
-        functools.partial(update_kernel, chunk),
+        update_kernel,
         out_shape=jax.ShapeDtypeStruct((places, channels), jnp.bfloat16),
         in_specs=[in_vmem] * 4,
-        out_specs=in_hbm,
-        scratch_shapes=[
-            pltpu.VMEM((places, channels), jnp.bfloat16),
-            pltpu.SemaphoreType.DMA((places // chunk,)),
-        ],
+        out_specs=in_vmem,
         compiler_params=pltpu.CompilerParams(vmem_limit_bytes=vmem_bytes),
         name="update",
-    )(triangle, gating, columns, w_out)
+    )(triangle, gating, columns, w_out_t)
 
 
 def make_triangle(sides, shifts, rows, loops, local_rows, local_cols):
@@ -338,16 +278,25 @@
     places = local_rows * local_cols
 
     pair = pair.reshape(places, channels)
-    in_gain, in_bias = ln_in_gain[None], ln_in_bias[None]
-    sides = make_sides(pair, in_gain, in_bias, w_proj, devices)
-    sides = sides.reshape(devices, 2 * share, places)
-    gating, columns, w_out, shifts = make_prepared(
-        pair, in_gain, in_bias, w_gate, ln_out_gain[None], ln_out_bias[None], w_out, sides, local_rows, local_cols
+    sides, gating, columns, w_out_t, shifts = make_sides(
+        devices,
+        local_rows,
+        local_cols,
+        pair,
+        w_proj,
+        w_gate,
+        ln_in_gain[None],
+        ln_in_bias[None],
+        ln_out_gain[None],
+        ln_out_bias[None],
+        w_out,
     )
-    sides = lax.all_to_all(sides, axes, split_axis=0, concat_axis=0)
+    sides = lax.all_to_all(
+        sides.reshape(devices, 2 * share, places), axes, split_axis=0, concat_axis=0
+    )
     triangle = make_triangle(sides, shifts, rows, loops, local_rows, local_cols)
     triangle = lax.all_to_all(triangle, axes, split_axis=0, concat_axis=0)
-    update = make_update(triangle.reshape(hidden, places), gating, columns, w_out)
+    update = make_update(triangle.reshape(hidden, places), gating, columns, w_out_t)
     return update.reshape(local_rows, local_cols, channels)
 
 

time: 44.9 us -> 43.2 us (0.962)
  blocking collectives: 14.5 us -> 38.3 us
  waiting for transfers between devices: 15.4 us -> 0 us
  starting transfers between devices: 7.3 us -> 0 us
  Pallas kernels: 6.6 us -> 4.58 us
  local copies, waits for them, and re-layouts: 0.72 us -> 0.07 us
    all_to_all x0 -> x1, blocking collectives: none -> 23.8 us  [on_device(): lax.all_to_all(sides.reshape(devices, 2 * share, places), axes, split_axi...]
    all_to_all x1 -> x0, waiting for transfers between devices: 15.4 us -> none  [on_device(): sides = lax.all_to_all(sides, axes, split_axis=0, concat_axis=0)]
    all_to_all x1 -> x0, starting transfers between devices: 7.3 us -> none  [on_device(): sides = lax.all_to_all(sides, axes, split_axis=0, concat_axis=0)]
    pallas_call x3 -> x2, Pallas kernels: 5.4 us -> 3.37 us  [the longest x1 2.15 us: make_sides(): pl.pallas_call(functools.partial(sides_kernel, devices, offsets, local_co...]
    unnamed x16 -> x0, local copies, waits for them, and re-layouts: 0.64 us -> none
  transfers between devices with their start and end apart: 1 -> 0, of which waited for: 1 -> 0; matrix products, arithmetic and copies ran while one was open for 0% -> 0% of each run, Pallas kernels for 1% -> 0%
where the time goes in v4:
time: 43.2 us; the launch traced here: 43 us
  blocking collectives  38.3 us (89%)
  Pallas kernels  4.58 us (11%)
    all_to_all x1, blocking collectives, on_device(): lax.all_to_all(sides.reshape(devices, 2 * share, places), axes, split_axi...  23.8 us
    all_to_all x1, blocking collectives, on_device(): triangle = lax.all_to_all(triangle, axes, split_axis=0, concat_axis=0)  14.5 us
    pallas_call x1, Pallas kernels, make_sides(): pl.pallas_call(functools.partial(sides_kernel, devices, offsets, local_co...  2.15 us
    pallas_call x1, Pallas kernels, make_update(): pl.pallas_call(update_kernel, out_shape=jax.ShapeDtypeStruct((places, cha...  1.22 us
    pallas_call x1, Pallas kernels, make_triangle(): pl.pallas_call(kernel, out_shape=jax.ShapeDtypeStruct((devices, share, pl...  1.2 us

profile of v4, /device:TPU:0, one launch (start us, length us, event | category | flops | bytes accessed | tf_op | source)
XLA Modules:
  0.0 43.0 jit_solution(3566645008105732042)
XLA Ops:
  0.0 2.2 %sides.1 = (bf16[256,1152]{1,0:T(8,128)(2,1)S(1)}, f32[128,1152]{1,0:T(8,128)S(1)}, f32[2,128,128]{2,1,0:T(8,128)S(1)}, bf16[128,128]{1,0:T(8,128)(2,1)S(1)}, bf16[8,256,128]{2,1,0:T(8,128)(2,1)S(1)}) custom-call(bf16[1152,128]{1,0:T(8,128)(2,1)} %bitcast.8, bf16[128,512]{1,0:T(8,128)(2,1)} %refs_1_.1, bf16[128,128]{1,0:T(8,128)(2,1)} %refs_2_.1, ...), custom_call_target="tpu_custom_call" | custom-call | tf_op jit(solution)/shard_map/sides/pallas_call | solution.py:199
  2.2 23.8 %all_to_all.10.in_ref = bf16[32,8,1152]{2,1,0:T(8,128)(2,1)S(1)} all-to-all(bf16[32,8,1152]{2,1,0:T(8,128)(2,1)S(1)} %bitcast.7), channel_id=1, replica_groups=mesh['row'=8,'loop'=4] {'row','loop'}, dimensions={0} | all-to-all | bytes 1179648 | tf_op jit(solution)/shard_map/all_to_all | solution.py:294
  26.0 1.2 %triangle.1 = bf16[32,4,1152]{2,1,0:T(4,128)(2,1)S(1)} custom-call(bf16[32,8,1152]{2,1,0:T(8,128)(2,1)S(1)} %all_to_all.10.in_ref, bf16[8,256,128]{2,1,0:T(8,128)(2,1)S(1)} %get-tuple-element.11.shifts_ref), custom_call_target="tpu_custom_call" | custom-call | tf_op jit(solution)/shard_map/triangle/pallas_call | solution.py:259
  27.2 14.5 %all_to_all.11 = bf16[32,4,1152]{2,1,0:T(4,128)(2,1)S(1)} all-to-all(bf16[32,4,1152]{2,1,0:T(4,128)(2,1)S(1)} %triangle.1), channel_id=1, replica_groups=mesh['row'=8,'loop'=4] {'row','loop'}, dimensions={0} | all-to-all | bytes 589824 | tf_op jit(solution)/shard_map/all_to_all | solution.py:298
  41.7 0.1 reshape.14.tri_ref
  41.8 1.2 %update.1 = bf16[1152,128]{1,0:T(8,128)(2,1)} custom-call(bf16[128,1152]{1,0:T(8,128)(2,1)S(1)} %reshape.14.tri_ref, f32[128,1152]{1,0:T(8,128)S(1)} %get-tuple-element.12.gating_ref, f32[2,128,128]{2,1,0:T(8,128)S(1)} %get-tuple-element.13.columns_ref, bf16[128,128]{1,0:T(8,128)(2,1)S(1)} %get-tuple-element.14.w_ref), custom_call_target="tpu_custom_call" | custom-call | tf_op jit(solution)/shard_map/update/pallas_call | solution.py:227

commit v5 on v4

v5 whole, which is shorter than its diff:
```python
import functools
import math

import jax
import jax.numpy as jnp
from jax import lax
from jax.experimental import pallas as pl
from jax.experimental.pallas import tpu as pltpu
from jax.sharding import Mesh
from jax.sharding import PartitionSpec as P

epsilon = 1e-05
in_vmem = pl.BlockSpec(memory_space=pltpu.VMEM)
in_hbm = pl.BlockSpec(memory_space=pltpu.HBM)
vmem_bytes = 48 * 2**20


def line_offsets(local_rows, local_cols):
    return sorted({k * local_cols % 128 for k in range(local_rows)})


def line_tiles(local_cols):
    tiles = math.lcm(local_cols, 128) // 128
    return [(u * 128 // local_cols, ((u + 1) * 128 - 1) // local_cols) for u in range(tiles)]


def in_lines(rows, loops, share, local_rows, local_cols):
    return (
        local_cols <= 64
        and local_cols % local_rows == 0
        and local_rows % 8 == 0
        and local_rows % (math.lcm(local_cols, 128) // local_cols) == 0
        and loops % 2 == 0
        and rows * local_rows == loops * local_cols
        and share % 8 == 0
    )


def sides_kernel(owners, local_rows, local_cols, *refs):
    given, results, held, sems = refs[:8], refs[8:14], refs[14:22], refs[22]
    out_ref, gating_ref, columns_ref, w_out_t_ref, shifts_ref, returns_ref = results
    copies = [pltpu.make_async_copy(*ends, sems.at[n]) for n, ends in enumerate(zip(given, held))]
    for copy in copies:
        copy.start()
    pair_ref, w_proj_ref, w_gate_ref, in_gain_ref, in_bias_ref, out_gain_ref, out_bias_ref, w_out_ref = held
    wide = w_proj_ref.shape[1]
    half, hidden = wide // 2, wide // 4
    share = hidden // owners

    row = lax.broadcasted_iota(jnp.int32, (1, wide), 1)
    value, row = row // half, row % half
    owner, row = row // (2 * share), row % (2 * share)
    column = ((row // share) * 2 + value) * hidden + owner * share + row % share
    source = lax.broadcasted_iota(jnp.int32, (wide, wide), 0)
    pick = jnp.where(source == column, 1.0, 0.0).astype(jnp.bfloat16)

    source = lax.broadcasted_iota(jnp.int32, (256, 128), 0)
    lane = lax.broadcasted_iota(jnp.int32, (256, 128), 1)
    for n, offset in enumerate(line_offsets(local_rows, local_cols)):
        wanted = ((lane & 63) + offset) & 127
        wanted = jnp.where(lane >= 64, wanted + 128, wanted)
        picked = (source == wanted) & ((lane & 63) < local_cols)
        shifts_ref[n] = jnp.where(picked, 1.0, 0.0).astype(jnp.bfloat16)

    source = lax.broadcasted_iota(jnp.int32, (128, 256), 0)
    lane = lax.broadcasted_iota(jnp.int32, (128, 256), 1)
    begin = 0
    for u, (first, last) in enumerate(line_tiles(local_cols)):
        for k in range(first, last + 1):
            inside = (lane & 127) + (u * 128 - k * local_cols)
            wanted = jnp.where(lane >= 128, inside + 64, inside)
            picked = (source == wanted) & (inside >= 0) & (inside < local_cols)
            returns_ref[begin : begin + 128, :] = jnp.where(picked, 1.0, 0.0).astype(jnp.bfloat16)
            begin += 128

    for copy in copies:
        copy.wait()
    weights = jnp.dot(w_proj_ref[...], pick, preferred_element_type=jnp.float32).T.astype(jnp.bfloat16)
    weights = jnp.concatenate([weights, w_gate_ref[...].astype(jnp.float32).T.astype(jnp.bfloat16)], axis=0)
    values = pair_ref[...].astype(jnp.float32)
    center = values - jnp.mean(values, axis=-1, keepdims=True)
    spread = jnp.mean(center * center, axis=-1, keepdims=True)
    normed = center * lax.rsqrt(spread + epsilon) * in_gain_ref[...] + in_bias_ref[...]
    projected = lax.dot_general(
        weights, normed.astype(jnp.bfloat16), (((1,), (1,)), ((), ())), preferred_element_type=jnp.float32
    )
    sides = jax.nn.sigmoid(projected[:half]) * projected[half:wide]
    out_ref[...] = sides.astype(jnp.bfloat16)
    gating_ref[...] = jax.nn.sigmoid(projected[wide:])
    columns_ref[0] = jnp.broadcast_to(out_gain_ref[...], (128, hidden)).T
    columns_ref[1] = jnp.broadcast_to(out_bias_ref[...], (128, hidden)).T
    w_out_t_ref[...] = w_out_ref[...].astype(jnp.float32).T.astype(jnp.bfloat16)


def triangle_kernel(rows, inner, loops, local_rows, local_cols, pad, in_ref, out_ref, sides_ref, tri_ref):
    both = in_ref.shape[1]
    share = both // 2
    depth = inner * local_rows
    tiles = loops * pad // 128
    blank = jnp.zeros((both, pad - local_cols), jnp.float32)

    @pl.loop(0, inner)
    def unpack(r):
        blocks = [in_ref[r * loops + l].astype(jnp.float32) for l in range(loops)]
        for k in range(local_rows):
            line = []
            for block in blocks:
                line.append(block[:, k * local_cols : (k + 1) * local_cols])
                if pad > local_cols:
                    line.append(blank)
            line = jnp.concatenate(line, axis=1)
            for t in range(tiles):
                place = pl.ds(t * both * depth + r * local_rows + k, both, stride=depth)
                sides_ref[place, :] = line[:, t * 128 : (t + 1) * 128]

    def matrix(index):
        return jnp.concatenate(
            [sides_ref[pl.ds((t * both + index) * depth, depth), :] for t in range(tiles)], axis=1
        ).astype(jnp.bfloat16)

    for c in range(share):
        product = lax.dot_general(
            matrix(c), matrix(share + c), (((0,), (0,)), ((), ())), preferred_element_type=jnp.float32
        )
        for t in range(tiles):
            tri_ref[pl.ds((t * share + c) * loops * pad, loops * pad), :] = product[:, t * 128 : (t + 1) * 128]

    @pl.loop(0, rows)
    def pack(r):
        begin = r * local_rows
        begin = (begin // local_cols) * pad + begin % local_cols
        for l in range(loops):
            first, last = l * pad // 128, -(-(l * pad + local_cols) // 128)
            line = []
            for k in range(local_rows):
                here = [
                    tri_ref[pl.ds(t * share * loops * pad + begin + k, share, stride=loops * pad), :]
                    for t in range(first, last)
                ]
                offset = l * pad - first * 128
                line.append(jnp.concatenate(here, axis=1)[:, offset : offset + local_cols])
            out_ref[r * loops + l] = jnp.concatenate(line, axis=1).astype(jnp.bfloat16)


def line_triangle_kernel(inner, loops, local_rows, local_cols, in_ref, shifts_ref, returns_ref, out_ref, sides_ref, tri_ref):
    both = in_ref.shape[1]
    share = both // 2
    depth = inner * local_rows
    pairs = loops // 2
    group = local_cols // local_rows
    height = depth + 8
    block = loops * local_rows + 8
    lane = lax.broadcasted_iota(jnp.int32, (inner * both, 128), 1)

    blocks = [jnp.concatenate([in_ref[r * loops + l] for r in range(inner)], axis=0) for l in range(loops)]
    for n, offset in enumerate(line_offsets(local_rows, local_cols)):
        stack, target = [], []
        for pair in range(pairs):
            for k in range(local_rows):
                u = k * local_cols // 128
                if k * local_cols % 128 != offset:
                    continue
                line = []
                for side in blocks[2 * pair : 2 * pair + 2]:
                    tile = side[:, u * 128 : (u + 1) * 128]
                    if offset + local_cols > 128:
                        tile = jnp.where(lane >= offset, tile, side[:, (u + 1) * 128 : (u + 2) * 128])
                    line.append(tile)
                stack.append(jnp.concatenate(line, axis=1))
                target.append(pair * both * height + k)
        lines = jnp.dot(jnp.concatenate(stack, axis=0), shifts_ref[n], preferred_element_type=jnp.float32)
        for m, place in enumerate(target):
            for r in range(inner):
                for part in range(0, both, 8):
                    first = (m * inner + r) * both + part
                    target_rows = pl.ds(place + part * height + r * local_rows, 8, stride=height)
                    sides_ref[target_rows, :] = lines[first : first + 8]

    def matrix(index):
        return jnp.concatenate(
            [sides_ref[pl.ds((t * both + index) * height, depth), :] for t in range(pairs)], axis=1
        ).astype(jnp.bfloat16)

    for c in range(share):
        product = lax.dot_general(
            matrix(c), matrix(share + c), (((0,), (0,)), ((), ())), preferred_element_type=jnp.float32
        )
        for t in range(pairs):
            for h in range(group):
                for l in range(loops):
                    place = ((t * group + h) * share + c) * block + l * local_rows
                    first = l * 64 + h * local_rows
                    tri_ref[place : place + local_rows, :] = product[
                        first : first + local_rows, t * 128 : (t + 1) * 128
                    ]

    members = group * share
    period = math.lcm(local_cols, 128) // local_cols
    tiles = line_tiles(local_cols)
    for t in range(pairs):

        def tri_line(l, k):
            parts = [
                tri_ref[pl.ds((t * members + part) * block + l * local_rows + k, 8, stride=block), :]
                for part in range(0, members, 8)
            ]
            return jnp.concatenate(parts, axis=0).astype(jnp.bfloat16)

        begin = 0
        for u, (first, last) in enumerate(tiles):
            stack = [
                jnp.concatenate([tri_line(l, turn + k) for k in range(first, last + 1)], axis=1)
                for l in range(loops)
                for turn in range(0, local_rows, period)
            ]
            end = begin + (last + 1 - first) * 128
            lanes = jnp.dot(
                jnp.concatenate(stack, axis=0), returns_ref[begin:end, :], preferred_element_type=jnp.float32
            ).astype(jnp.bfloat16)
            begin = end
            for l in range(loops):
                for turn in range(local_rows // period):
                    place = (turn * len(tiles) + u) * 128
                    for h in range(group):
                        row = ((l * (local_rows // period) + turn) * group + h) * share
                        for side in range(2):
                            out_ref[(l * group + h) * loops + 2 * t + side, :, place : place + 128] = lanes[
                                row : row + share, side * 128 : (side + 1) * 128
                            ]


def make_sides(owners, local_rows, local_cols, *given):
    places, channels = given[0].shape
    wide = given[1].shape[1]
    hidden = wide // 4
    returns = sum(last + 1 - first for first, last in line_tiles(local_cols))
    return pl.pallas_call(
        functools.partial(sides_kernel, owners, local_rows, local_cols),
        out_shape=(
            jax.ShapeDtypeStruct((wide // 2, places), jnp.bfloat16),
            jax.ShapeDtypeStruct((channels, places), jnp.float32),
            jax.ShapeDtypeStruct((2, hidden, 128), jnp.float32),
            jax.ShapeDtypeStruct((channels, hidden), jnp.bfloat16),
            jax.ShapeDtypeStruct((len(line_offsets(local_rows, local_cols)), 256, 128), jnp.bfloat16),
            jax.ShapeDtypeStruct((returns * 128, 256), jnp.bfloat16),
        ),
        in_specs=[in_hbm] * len(given),
        out_specs=[in_vmem] * 6,
        scratch_shapes=[pltpu.VMEM(x.shape, x.dtype) for x in given] + [pltpu.SemaphoreType.DMA((len(given),))],
        compiler_params=pltpu.CompilerParams(vmem_limit_bytes=vmem_bytes),
        name="sides",
    )(*[pltpu.with_memory_space_constraint(x, pltpu.HBM) for x in given])


def update_kernel(tri_ref, gating_ref, columns_ref, w_ref, out_ref):
    values = tri_ref[0].astype(jnp.float32)
    for half in range(1, tri_ref.shape[0]):
        values += tri_ref[half].astype(jnp.float32)
    center = values - jnp.mean(values, axis=0, keepdims=True)
    spread = jnp.mean(center * center, axis=0, keepdims=True)
    mixed = center * lax.rsqrt(spread + epsilon) * columns_ref[0][:, :1] + columns_ref[1][:, :1]
    outgoing = jnp.dot(w_ref[...], mixed.astype(jnp.bfloat16), preferred_element_type=jnp.float32)
    out_ref[...] = (gating_ref[...] * outgoing).T.astype(jnp.bfloat16)


def make_update(triangle, gating, columns, w_out_t):
    channels, places = gating.shape
    return pl.pallas_call(
        update_kernel,
        out_shape=jax.ShapeDtypeStruct((places, channels), jnp.bfloat16),
        in_specs=[in_vmem] * 4,
        out_specs=in_vmem,
        compiler_params=pltpu.CompilerParams(vmem_limit_bytes=vmem_bytes),
        name="update",
    )(triangle, gating, columns, w_out_t)


def make_triangle(sides, shifts, returns, rows, inner, loops, local_rows, local_cols):
    owners, both, places = sides.shape
    share = both // 2
    operands = [sides]
    if in_lines(rows, loops, share, local_rows, local_cols):
        operands += [shifts, returns]
        kernel = functools.partial(line_triangle_kernel, inner, loops, local_rows, local_cols)
        sides_rows = (loops // 2 * both + 1) * (inner * local_rows + 8)
        tri_rows = (loops // 2 * share * (local_cols // local_rows) + 1) * (loops * local_rows + 8)
    else:
        pad = 64 if local_cols <= 64 and loops % 2 == 0 else -(-local_cols // 128) * 128
        kernel = functools.partial(triangle_kernel, rows, inner, loops, local_rows, local_cols, pad)
        sides_rows = loops * pad // 128 * both * inner * local_rows
        tri_rows = loops * pad // 128 * share * loops * pad
    return pl.pallas_call(
        kernel,
        out_shape=jax.ShapeDtypeStruct((rows * loops, share, places), jnp.bfloat16),
        in_specs=[in_vmem] * len(operands),
        out_specs=in_vmem,
        scratch_shapes=[
            pltpu.VMEM((sides_rows, 128), jnp.float32),
            pltpu.VMEM((tri_rows, 128), jnp.float32),
        ],
        compiler_params=pltpu.CompilerParams(vmem_limit_bytes=vmem_bytes),
        name="triangle",
    )(*operands)


def on_device(halves, inner, loops, pair, ln_in_gain, ln_in_bias, w_proj, w_gate, ln_out_gain, ln_out_bias, w_out):
    local_rows, local_cols, channels = pair.shape
    hidden = w_out.shape[0]
    owners = inner * loops
    share = hidden // owners
    places = local_rows * local_cols

    sides, gating, columns, w_out_t, shifts, returns = make_sides(
        owners,
        local_rows,
        local_cols,
        pair.reshape(places, channels),
        w_proj,
        w_gate,
        ln_in_gain[None],
        ln_in_bias[None],
        ln_out_gain[None],
        ln_out_bias[None],
        w_out,
    )
    sides = lax.all_to_all(
        sides.reshape(owners, 2 * share, places), ("inner", "loop"), split_axis=0, concat_axis=0
    )
    triangle = make_triangle(
        sides, shifts, returns, halves * inner, inner, loops, local_rows, local_cols
    )
    triangle = lax.all_to_all(triangle, ("half", "inner", "loop"), split_axis=0, concat_axis=0)
    update = make_update(triangle.reshape(halves, hidden, places), gating, columns, w_out_t)
    return update.reshape(local_rows, local_cols, channels)


def solution(mesh):
    rows, loops = mesh.shape["row"], mesh.shape["loop"]
    halves = 2 if rows % 2 == 0 else 1
    inner = rows // halves
    split = Mesh(mesh.devices.reshape(halves, inner, loops), ("half", "inner", "loop"))
    placed = P(("half", "inner"), "loop", None)
    return jax.shard_map(
        lambda *arrays: on_device(halves, inner, loops, *arrays),
        mesh=split,
        in_specs=(placed, P(), P(), P(), P(), P(), P(), P()),
        out_specs=placed,
        check_vma=False,
    )
```

time: 43.2 us -> 42.1 us (0.975)
  blocking collectives: 38.3 us -> 37.1 us
    all_to_all x2, blocking collectives: 38.3 us -> 37.1 us  [the longest x1 19.7 us: on_device(): lax.all_to_all(triangle, ('half', 'inner', 'loop'), split_axis=0, concat_...]
where the time goes in v5:
time: 42.1 us; the launch traced here: 41.9 us
  blocking collectives  37.1 us (88%)
  Pallas kernels  4.85 us (12%)
    all_to_all x1, blocking collectives, on_device(): lax.all_to_all(triangle, ('half', 'inner', 'loop'), split_axis=0, concat_...  19.7 us
    all_to_all x1, blocking collectives, on_device(): lax.all_to_all(sides.reshape(owners, 2 * share, places), ('inner', 'loop'...  17.3 us
    pallas_call x1, Pallas kernels, make_sides(): pl.pallas_call(functools.partial(sides_kernel, owners, local_rows, local_...  2.15 us
    pallas_call x1, Pallas kernels, make_triangle(): pl.pallas_call(kernel, out_shape=jax.ShapeDtypeStruct((rows * loops, shar...  1.46 us
    pallas_call x1, Pallas kernels, make_update(): pl.pallas_call(update_kernel, out_shape=jax.ShapeDtypeStruct((places, cha...  1.24 us

profile of v5, /device:TPU:0, one launch (start us, length us, event | category | flops | bytes accessed | tf_op | source)
XLA Modules:
  0.0 41.9 jit_solution(12933194931734980223)
XLA Ops:
  0.0 2.2 %sides.1 = (bf16[256,1152]{1,0:T(8,128)(2,1)S(1)}, f32[128,1152]{1,0:T(8,128)S(1)}, f32[2,128,128]{2,1,0:T(8,128)S(1)}, bf16[128,128]{1,0:T(8,128)(2,1)S(1)}, bf...) custom-call(bf16[1152,128]{1,0:T(8,128)(2,1)} %bitcast.10, bf16[128,512]{1,0:T(8,128)(2,1)} %refs_1_.1, ...), custom_call_target="tpu_custom_call" | custom-call | tf_op jit(solution)/shard_map/sides/pallas_call | solution.py:237
  2.2 17.3 %all_to_all.10.in_ref = bf16[16,16,1152]{2,1,0:T(8,128)(2,1)S(1)} all-to-all(bf16[16,16,1152]{2,1,0:T(8,128)(2,1)S(1)} %bitcast.9), channel_id=1, replica_groups=mesh['half'=2,'inner'=4,'loop'=4] {'inner','loop'}, dimensions={0} | all-to-all | bytes 1179648 | tf_op jit(solution)/shard_map/all_to_all | solution.py:326
  19.5 1.5 %triangle.1 = bf16[32,8,1152]{2,1,0:T(8,128)(2,1)S(1)} custom-call(bf16[16,16,1152]{2,1,0:T(8,128)(2,1)S(1)} %all_to_all.10.in_ref, bf16[8,256,128]{2,1,0:T(8,128)(2,1)S(1)} %get-tuple-element.12.shifts_ref, bf16[1280,256]{1,0:T(8,128)(2,1)S(1)} %get-tuple-element.13.returns_ref), custom_call_target="tpu_custom_call" | custom-call | tf_op jit(solution)/shard_map/triangle/pallas_call | solution.py:292
  21.0 19.7 %all_to_all.11 = bf16[32,8,1152]{2,1,0:T(8,128)(2,1)S(1)} all-to-all(bf16[32,8,1152]{2,1,0:T(8,128)(2,1)S(1)} %triangle.1), channel_id=1, replica_groups=mesh['half'=2,'inner'=4,'loop'=4] {'half','inner','loop'}, dimensions={0} | all-to-all | bytes 1179648 | tf_op jit(solution)/shard_map/all_to_all | solution.py:332
  40.7 1.2 %update.1 = bf16[1152,128]{1,0:T(8,128)(2,1)} custom-call(bf16[2,128,1152]{2,1,0:T(8,128)(2,1)S(1)} %bitcast.8, f32[128,1152]{1,0:T(8,128)S(1)} %get-tuple-element.14.gating_ref, f32[2,128,128]{2,1,0:T(8,128)S(1)} %get-tuple-element.15.columns_ref, bf16[128,128]{1,0:T(8,128)(2,1)S(1)} %get-tuple-element.16.w_ref), custom_call_target="tpu_custom_call" | custom-call | tf_op jit(solution)/shard_map/update/pallas_call | solution.py:268

commit v6 on v5

--- a/solution.py
+++ b/solution.py
@@ -15,8 +15,16 @@
 vmem_bytes = 48 * 2**20
 
 
-def line_offsets(local_rows, local_cols):
-    return sorted({k * local_cols % 128 for k in range(local_rows)})
+def line_groups(local_cols):
+    groups = []
+    for k in range(math.lcm(local_cols, 128) // local_cols):
+        tile, offset = divmod(k * local_cols, 128)
+        over = offset + local_cols > 128
+        if over or not groups or groups[-1][0] != tile:
+            groups.append((tile, k, 1))
+        else:
+            groups[-1] = (tile, groups[-1][1], groups[-1][2] + 1)
+    return groups
 
 
 def line_tiles(local_cols):
@@ -36,7 +44,7 @@
     )
 
 
-def sides_kernel(owners, local_rows, local_cols, *refs):
+def sides_kernel(owners, local_cols, *refs):
     given, results, held, sems = refs[:8], refs[8:14], refs[14:22], refs[22]
     out_ref, gating_ref, columns_ref, w_out_t_ref, shifts_ref, returns_ref = results
     copies = [pltpu.make_async_copy(*ends, sems.at[n]) for n, ends in enumerate(zip(given, held))]
@@ -56,11 +64,11 @@
 
     source = lax.broadcasted_iota(jnp.int32, (256, 128), 0)
     lane = lax.broadcasted_iota(jnp.int32, (256, 128), 1)
-    for n, offset in enumerate(line_offsets(local_rows, local_cols)):
-        wanted = ((lane & 63) + offset) & 127
+    for k in range(shifts_ref.shape[1] // 128):
+        wanted = ((lane & 63) + k * local_cols % 128) & 127
         wanted = jnp.where(lane >= 64, wanted + 128, wanted)
         picked = (source == wanted) & ((lane & 63) < local_cols)
-        shifts_ref[n] = jnp.where(picked, 1.0, 0.0).astype(jnp.bfloat16)
+        shifts_ref[:, k * 128 : (k + 1) * 128] = jnp.where(picked, 1.0, 0.0).astype(jnp.bfloat16)
 
     source = lax.broadcasted_iota(jnp.int32, (128, 256), 0)
     lane = lax.broadcasted_iota(jnp.int32, (128, 256), 1)
@@ -153,28 +161,34 @@
     lane = lax.broadcasted_iota(jnp.int32, (inner * both, 128), 1)
 
     blocks = [jnp.concatenate([in_ref[r * loops + l] for r in range(inner)], axis=0) for l in range(loops)]
-    for n, offset in enumerate(line_offsets(local_rows, local_cols)):
+    period = math.lcm(local_cols, 128) // local_cols
+    tiles = line_tiles(local_cols)
+    for u, k, count in line_groups(local_cols):
+        offset = k * local_cols % 128
         stack, target = [], []
         for pair in range(pairs):
-            for k in range(local_rows):
-                u = k * local_cols // 128
-                if k * local_cols % 128 != offset:
-                    continue
+            for turn in range(local_rows // period):
                 line = []
                 for side in blocks[2 * pair : 2 * pair + 2]:
-                    tile = side[:, u * 128 : (u + 1) * 128]
+                    at = (turn * len(tiles) + u) * 128
+                    tile = side[:, at : at + 128]
                     if offset + local_cols > 128:
-                        tile = jnp.where(lane >= offset, tile, side[:, (u + 1) * 128 : (u + 2) * 128])
+                        tile = jnp.where(lane >= offset, tile, side[:, at + 128 : at + 256])
                     line.append(tile)
                 stack.append(jnp.concatenate(line, axis=1))
-                target.append(pair * both * height + k)
-        lines = jnp.dot(jnp.concatenate(stack, axis=0), shifts_ref[n], preferred_element_type=jnp.float32)
+                target.append(pair * both * height + turn * period + k)
+        lines = jnp.dot(
+            jnp.concatenate(stack, axis=0),
+            shifts_ref[:, k * 128 : (k + count) * 128],
+            preferred_element_type=jnp.float32,
+        )
         for m, place in enumerate(target):
             for r in range(inner):
                 for part in range(0, both, 8):
                     first = (m * inner + r) * both + part
-                    target_rows = pl.ds(place + part * height + r * local_rows, 8, stride=height)
-                    sides_ref[target_rows, :] = lines[first : first + 8]
+                    for n in range(count):
+                        target_rows = pl.ds(place + part * height + r * local_rows + n, 8, stride=height)
+                        sides_ref[target_rows, :] = lines[first : first + 8, n * 128 : (n + 1) * 128]
 
     def matrix(index):
         return jnp.concatenate(
@@ -195,8 +209,6 @@
                     ]
 
     members = group * share
-    period = math.lcm(local_cols, 128) // local_cols
-    tiles = line_tiles(local_cols)
     for t in range(pairs):
 
         def tri_line(l, k):
@@ -229,19 +241,19 @@
                             ]
 
 
-def make_sides(owners, local_rows, local_cols, *given):
+def make_sides(owners, local_cols, *given):
     places, channels = given[0].shape
     wide = given[1].shape[1]
     hidden = wide // 4
     returns = sum(last + 1 - first for first, last in line_tiles(local_cols))
     return pl.pallas_call(
-        functools.partial(sides_kernel, owners, local_rows, local_cols),
+        functools.partial(sides_kernel, owners, local_cols),
         out_shape=(
             jax.ShapeDtypeStruct((wide // 2, places), jnp.bfloat16),
             jax.ShapeDtypeStruct((channels, places), jnp.float32),
             jax.ShapeDtypeStruct((2, hidden, 128), jnp.float32),
             jax.ShapeDtypeStruct((channels, hidden), jnp.bfloat16),
-            jax.ShapeDtypeStruct((len(line_offsets(local_rows, local_cols)), 256, 128), jnp.bfloat16),
+            jax.ShapeDtypeStruct((256, math.lcm(local_cols, 128) // local_cols * 128), jnp.bfloat16),
             jax.ShapeDtypeStruct((returns * 128, 256), jnp.bfloat16),
         ),
         in_specs=[in_hbm] * len(given),
@@ -312,7 +324,6 @@
 
     sides, gating, columns, w_out_t, shifts, returns = make_sides(
         owners,
-        local_rows,
         local_cols,
         pair.reshape(places, channels),
         w_proj,

time: 42.1 us -> 42.1 us (level)
  no operation moved by 1% of the time
where the time goes in v6:
time: 42.1 us; the launch traced here: 41.9 us
  blocking collectives  37.1 us (88%)
  Pallas kernels  4.8 us (11%)
    all_to_all x1, blocking collectives, on_device(): lax.all_to_all(triangle, ('half', 'inner', 'loop'), split_axis=0, concat_...  19.7 us
    all_to_all x1, blocking collectives, on_device(): lax.all_to_all(sides.reshape(owners, 2 * share, places), ('inner', 'loop'...  17.3 us
    pallas_call x1, Pallas kernels, make_sides(): pl.pallas_call(functools.partial(sides_kernel, owners, local_cols), out_s...  2.15 us
    pallas_call x1, Pallas kernels, make_triangle(): pl.pallas_call(kernel, out_shape=jax.ShapeDtypeStruct((rows * loops, shar...  1.41 us
    pallas_call x1, Pallas kernels, make_update(): pl.pallas_call(update_kernel, out_shape=jax.ShapeDtypeStruct((places, cha...  1.24 us

profile of v6, /device:TPU:0, one launch (start us, length us, event | category | flops | bytes accessed | tf_op | source)
XLA Modules:
  0.0 41.9 jit_solution(15913429978272580694)
XLA Ops:
  0.0 2.2 %sides.1 = (bf16[256,1152]{1,0:T(8,128)(2,1)S(1)}, f32[128,1152]{1,0:T(8,128)S(1)}, f32[2,128,128]{2,1,0:T(8,128)S(1)}, bf16[128,128]{1,0:T(8,128)(2,1)S(1)}, bf...) custom-call(bf16[1152,128]{1,0:T(8,128)(2,1)} %bitcast.10, bf16[128,512]{1,0:T(8,128)(2,1)} %refs_1_.1, ...), custom_call_target="tpu_custom_call" | custom-call | tf_op jit(solution)/shard_map/sides/pallas_call | solution.py:249
  2.2 17.3 %all_to_all.10.in_ref = bf16[16,16,1152]{2,1,0:T(8,128)(2,1)S(1)} all-to-all(bf16[16,16,1152]{2,1,0:T(8,128)(2,1)S(1)} %bitcast.9), channel_id=1, replica_groups=mesh['half'=2,'inner'=4,'loop'=4] {'inner','loop'}, dimensions={0} | all-to-all | bytes 1179648 | tf_op jit(solution)/shard_map/all_to_all | solution.py:337
  19.5 1.4 %triangle.1 = bf16[32,8,1152]{2,1,0:T(8,128)(2,1)S(1)} custom-call(bf16[16,16,1152]{2,1,0:T(8,128)(2,1)S(1)} %all_to_all.10.in_ref, bf16[256,1024]{1,0:T(8,128)(2,1)S(1)} %get-tuple-element.12.shifts_ref, bf16[1280,256]{1,0:T(8,128)(2,1)S(1)} %get-tuple-element.13.returns_ref), custom_call_target="tpu_custom_call" | custom-call | tf_op jit(solution)/shard_map/triangle/pallas_call | solution.py:304
  20.9 19.7 %all_to_all.11 = bf16[32,8,1152]{2,1,0:T(8,128)(2,1)S(1)} all-to-all(bf16[32,8,1152]{2,1,0:T(8,128)(2,1)S(1)} %triangle.1), channel_id=1, replica_groups=mesh['half'=2,'inner'=4,'loop'=4] {'half','inner','loop'}, dimensions={0} | all-to-all | bytes 1179648 | tf_op jit(solution)/shard_map/all_to_all | solution.py:343
  40.6 1.2 %update.1 = bf16[1152,128]{1,0:T(8,128)(2,1)} custom-call(bf16[2,128,1152]{2,1,0:T(8,128)(2,1)S(1)} %bitcast.8, f32[128,1152]{1,0:T(8,128)S(1)} %get-tuple-element.14.gating_ref, f32[2,128,128]{2,1,0:T(8,128)S(1)} %get-tuple-element.15.columns_ref, bf16[128,128]{1,0:T(8,128)(2,1)S(1)} %get-tuple-element.16.w_ref), custom_call_target="tpu_custom_call" | custom-call | tf_op jit(solution)/shard_map/update/pallas_call | solution.py:280

commit v7 on v6

--- a/solution.py
+++ b/solution.py
@@ -51,16 +51,8 @@
     for copy in copies:
         copy.start()
     pair_ref, w_proj_ref, w_gate_ref, in_gain_ref, in_bias_ref, out_gain_ref, out_bias_ref, w_out_ref = held
-    wide = w_proj_ref.shape[1]
-    half, hidden = wide // 2, wide // 4
+    hidden = w_proj_ref.shape[1] // 4
     share = hidden // owners
-
-    row = lax.broadcasted_iota(jnp.int32, (1, wide), 1)
-    value, row = row // half, row % half
-    owner, row = row // (2 * share), row % (2 * share)
-    column = ((row // share) * 2 + value) * hidden + owner * share + row % share
-    source = lax.broadcasted_iota(jnp.int32, (wide, wide), 0)
-    pick = jnp.where(source == column, 1.0, 0.0).astype(jnp.bfloat16)
 
     source = lax.broadcasted_iota(jnp.int32, (256, 128), 0)
     lane = lax.broadcasted_iota(jnp.int32, (256, 128), 1)
@@ -83,18 +75,21 @@
 
     for copy in copies:
         copy.wait()
-    weights = jnp.dot(w_proj_ref[...], pick, preferred_element_type=jnp.float32).T.astype(jnp.bfloat16)
-    weights = jnp.concatenate([weights, w_gate_ref[...].astype(jnp.float32).T.astype(jnp.bfloat16)], axis=0)
     values = pair_ref[...].astype(jnp.float32)
     center = values - jnp.mean(values, axis=-1, keepdims=True)
     spread = jnp.mean(center * center, axis=-1, keepdims=True)
     normed = center * lax.rsqrt(spread + epsilon) * in_gain_ref[...] + in_bias_ref[...]
-    projected = lax.dot_general(
-        weights, normed.astype(jnp.bfloat16), (((1,), (1,)), ((), ())), preferred_element_type=jnp.float32
-    )
-    sides = jax.nn.sigmoid(projected[:half]) * projected[half:wide]
-    out_ref[...] = sides.astype(jnp.bfloat16)
-    gating_ref[...] = jax.nn.sigmoid(projected[wide:])
+    normed = normed.astype(jnp.bfloat16)
+    projected, gate = [
+        lax.dot_general(weights[...], normed, (((0,), (1,)), ((), ())), preferred_element_type=jnp.float32)
+        for weights in (w_proj_ref, w_gate_ref)
+    ]
+    left_gate, left, right_gate, right = [projected[n * hidden : (n + 1) * hidden] for n in range(4)]
+    left = jax.nn.sigmoid(left_gate) * left
+    right = jax.nn.sigmoid(right_gate) * right
+    sides = [side[at : at + share] for at in range(0, hidden, share) for side in (left, right)]
+    out_ref[...] = jnp.concatenate(sides, axis=0).astype(jnp.bfloat16)
+    gating_ref[...] = jax.nn.sigmoid(gate)
     columns_ref[0] = jnp.broadcast_to(out_gain_ref[...], (128, hidden)).T
     columns_ref[1] = jnp.broadcast_to(out_bias_ref[...], (128, hidden)).T
     w_out_t_ref[...] = w_out_ref[...].astype(jnp.float32).T.astype(jnp.bfloat16)

time: 42.1 us -> 41.9 us (level)
  no operation moved by 1% of the time
where the time goes in v7:
time: 41.9 us; the launch traced here: 41.7 us
  blocking collectives  37.1 us (89%)
  Pallas kernels  4.64 us (11%)
    all_to_all x1, blocking collectives, on_device(): lax.all_to_all(triangle, ('half', 'inner', 'loop'), split_axis=0, concat_...  19.7 us
    all_to_all x1, blocking collectives, on_device(): lax.all_to_all(sides.reshape(owners, 2 * share, places), ('inner', 'loop'...  17.3 us
    pallas_call x1, Pallas kernels, make_sides(): pl.pallas_call(functools.partial(sides_kernel, owners, local_cols), out_s...  1.98 us
    pallas_call x1, Pallas kernels, make_triangle(): pl.pallas_call(kernel, out_shape=jax.ShapeDtypeStruct((rows * loops, shar...  1.41 us
    pallas_call x1, Pallas kernels, make_update(): pl.pallas_call(update_kernel, out_shape=jax.ShapeDtypeStruct((places, cha...  1.24 us

profile of v7, /device:TPU:0, one launch (start us, length us, event | category | flops | bytes accessed | tf_op | source)
XLA Modules:
  0.0 41.7 jit_solution(10132721866974486514)
XLA Ops:
  0.0 2.0 %sides.1 = (bf16[256,1152]{1,0:T(8,128)(2,1)S(1)}, f32[128,1152]{1,0:T(8,128)S(1)}, f32[2,128,128]{2,1,0:T(8,128)S(1)}, bf16[128,128]{1,0:T(8,128)(2,1)S(1)}, bf...) custom-call(bf16[1152,128]{1,0:T(8,128)(2,1)} %bitcast.10, bf16[128,512]{1,0:T(8,128)(2,1)} %refs_1_.1, ...), custom_call_target="tpu_custom_call" | custom-call | tf_op jit(solution)/shard_map/sides/pallas_call | solution.py:244
  2.0 17.3 %all_to_all.10.in_ref = bf16[16,16,1152]{2,1,0:T(8,128)(2,1)S(1)} all-to-all(bf16[16,16,1152]{2,1,0:T(8,128)(2,1)S(1)} %bitcast.9), channel_id=1, replica_groups=mesh['half'=2,'inner'=4,'loop'=4] {'inner','loop'}, dimensions={0} | all-to-all | bytes 1179648 | tf_op jit(solution)/shard_map/all_to_all | solution.py:332
  19.3 1.4 %triangle.1 = bf16[32,8,1152]{2,1,0:T(8,128)(2,1)S(1)} custom-call(bf16[16,16,1152]{2,1,0:T(8,128)(2,1)S(1)} %all_to_all.10.in_ref, bf16[256,1024]{1,0:T(8,128)(2,1)S(1)} %get-tuple-element.12.shifts_ref, bf16[1280,256]{1,0:T(8,128)(2,1)S(1)} %get-tuple-element.13.returns_ref), custom_call_target="tpu_custom_call" | custom-call | tf_op jit(solution)/shard_map/triangle/pallas_call | solution.py:299
  20.8 19.7 %all_to_all.11 = bf16[32,8,1152]{2,1,0:T(8,128)(2,1)S(1)} all-to-all(bf16[32,8,1152]{2,1,0:T(8,128)(2,1)S(1)} %triangle.1), channel_id=1, replica_groups=mesh['half'=2,'inner'=4,'loop'=4] {'half','inner','loop'}, dimensions={0} | all-to-all | bytes 1179648 | tf_op jit(solution)/shard_map/all_to_all | solution.py:338
  40.5 1.2 %update.1 = bf16[1152,128]{1,0:T(8,128)(2,1)} custom-call(bf16[2,128,1152]{2,1,0:T(8,128)(2,1)S(1)} %bitcast.8, f32[128,1152]{1,0:T(8,128)S(1)} %get-tuple-element.14.gating_ref, f32[2,128,128]{2,1,0:T(8,128)S(1)} %get-tuple-element.15.columns_ref, bf16[128,128]{1,0:T(8,128)(2,1)S(1)} %get-tuple-element.16.w_ref), custom_call_target="tpu_custom_call" | custom-call | tf_op jit(solution)/shard_map/update/pallas_call | solution.py:275

commit v8 on v7

--- a/solution.py
+++ b/solution.py
@@ -145,7 +145,7 @@
             out_ref[r * loops + l] = jnp.concatenate(line, axis=1).astype(jnp.bfloat16)
 
 
-def line_triangle_kernel(inner, loops, local_rows, local_cols, in_ref, shifts_ref, returns_ref, out_ref, sides_ref, tri_ref):
+def line_triangle_kernel(inner, loops, local_rows, local_cols, in_ref, shifts_ref, returns_ref, out_ref, sides_ref, *tri_refs):
     both = in_ref.shape[1]
     share = both // 2
     depth = inner * local_rows
@@ -190,25 +190,24 @@
             [sides_ref[pl.ds((t * both + index) * height, depth), :] for t in range(pairs)], axis=1
         ).astype(jnp.bfloat16)
 
-    for c in range(share):
-        product = lax.dot_general(
-            matrix(c), matrix(share + c), (((0,), (0,)), ((), ())), preferred_element_type=jnp.float32
-        )
-        for t in range(pairs):
+    for t in range(pairs):
+        for c in range(share):
+            right = sides_ref[pl.ds((t * both + share + c) * height, depth), :].astype(jnp.bfloat16)
+            product = lax.dot_general(
+                matrix(c), right, (((0,), (0,)), ((), ())), preferred_element_type=jnp.float32
+            )
             for h in range(group):
                 for l in range(loops):
-                    place = ((t * group + h) * share + c) * block + l * local_rows
+                    place = (h * share + c) * block + l * local_rows
                     first = l * 64 + h * local_rows
-                    tri_ref[place : place + local_rows, :] = product[
-                        first : first + local_rows, t * 128 : (t + 1) * 128
-                    ]
+                    tri_refs[t][place : place + local_rows, :] = product[first : first + local_rows, :]
 
     members = group * share
     for t in range(pairs):
 
         def tri_line(l, k):
             parts = [
-                tri_ref[pl.ds((t * members + part) * block + l * local_rows + k, 8, stride=block), :]
+                tri_refs[t][pl.ds(part * block + l * local_rows + k, 8, stride=block), :]
                 for part in range(0, members, 8)
             ]
             return jnp.concatenate(parts, axis=0).astype(jnp.bfloat16)
@@ -290,21 +289,18 @@
         operands += [shifts, returns]
         kernel = functools.partial(line_triangle_kernel, inner, loops, local_rows, local_cols)
         sides_rows = (loops // 2 * both + 1) * (inner * local_rows + 8)
-        tri_rows = (loops // 2 * share * (local_cols // local_rows) + 1) * (loops * local_rows + 8)
+        tri_rows = [(share * (local_cols // local_rows) + 1) * (loops * local_rows + 8)] * (loops // 2)
     else:
         pad = 64 if local_cols <= 64 and loops % 2 == 0 else -(-local_cols // 128) * 128
         kernel = functools.partial(triangle_kernel, rows, inner, loops, local_rows, local_cols, pad)
         sides_rows = loops * pad // 128 * both * inner * local_rows
-        tri_rows = loops * pad // 128 * share * loops * pad
+        tri_rows = [loops * pad // 128 * share * loops * pad]
     return pl.pallas_call(
         kernel,
         out_shape=jax.ShapeDtypeStruct((rows * loops, share, places), jnp.bfloat16),
         in_specs=[in_vmem] * len(operands),
         out_specs=in_vmem,
-        scratch_shapes=[
-            pltpu.VMEM((sides_rows, 128), jnp.float32),
-            pltpu.VMEM((tri_rows, 128), jnp.float32),
-        ],
+        scratch_shapes=[pltpu.VMEM((n, 128), jnp.float32) for n in [sides_rows] + tri_rows],
         compiler_params=pltpu.CompilerParams(vmem_limit_bytes=vmem_bytes),
         name="triangle",
     )(*operands)

time: 41.9 us -> 41.8 us (level)
  no operation moved by 1% of the time
where the time goes in v8:
time: 41.8 us; the launch traced here: 41.6 us
  blocking collectives  37.1 us (89%)
  Pallas kernels  4.55 us (11%)
    all_to_all x1, blocking collectives, on_device(): lax.all_to_all(triangle, ('half', 'inner', 'loop'), split_axis=0, concat_...  19.7 us
    all_to_all x1, blocking collectives, on_device(): lax.all_to_all(sides.reshape(owners, 2 * share, places), ('inner', 'loop'...  17.3 us
    pallas_call x1, Pallas kernels, make_sides(): pl.pallas_call(functools.partial(sides_kernel, owners, local_cols), out_s...  1.98 us
    pallas_call x1, Pallas kernels, make_triangle(): pl.pallas_call(kernel, out_shape=jax.ShapeDtypeStruct((rows * loops, shar...  1.33 us
    pallas_call x1, Pallas kernels, make_update(): pl.pallas_call(update_kernel, out_shape=jax.ShapeDtypeStruct((places, cha...  1.24 us

profile of v8, /device:TPU:0, one launch (start us, length us, event | category | flops | bytes accessed | tf_op | source)
XLA Modules:
  0.0 41.6 jit_solution(8316617081497494825)
XLA Ops:
  0.0 2.0 %sides.1 = (bf16[256,1152]{1,0:T(8,128)(2,1)S(1)}, f32[128,1152]{1,0:T(8,128)S(1)}, f32[2,128,128]{2,1,0:T(8,128)S(1)}, bf16[128,128]{1,0:T(8,128)(2,1)S(1)}, bf...) custom-call(bf16[1152,128]{1,0:T(8,128)(2,1)} %bitcast.10, bf16[128,512]{1,0:T(8,128)(2,1)} %refs_1_.1, ...), custom_call_target="tpu_custom_call" | custom-call | tf_op jit(solution)/shard_map/sides/pallas_call | solution.py:243
  2.0 17.3 %all_to_all.10.in_ref = bf16[16,16,1152]{2,1,0:T(8,128)(2,1)S(1)} all-to-all(bf16[16,16,1152]{2,1,0:T(8,128)(2,1)S(1)} %bitcast.9), channel_id=1, replica_groups=mesh['half'=2,'inner'=4,'loop'=4] {'inner','loop'}, dimensions={0} | all-to-all | bytes 1179648 | tf_op jit(solution)/shard_map/all_to_all | solution.py:328
  19.3 1.3 %triangle.1 = bf16[32,8,1152]{2,1,0:T(8,128)(2,1)S(1)} custom-call(bf16[16,16,1152]{2,1,0:T(8,128)(2,1)S(1)} %all_to_all.10.in_ref, bf16[256,1024]{1,0:T(8,128)(2,1)S(1)} %get-tuple-element.12.shifts_ref, bf16[1280,256]{1,0:T(8,128)(2,1)S(1)} %get-tuple-element.13.returns_ref), custom_call_target="tpu_custom_call" | custom-call | tf_op jit(solution)/shard_map/triangle/pallas_call | solution.py:298
  20.7 19.7 %all_to_all.11 = bf16[32,8,1152]{2,1,0:T(8,128)(2,1)S(1)} all-to-all(bf16[32,8,1152]{2,1,0:T(8,128)(2,1)S(1)} %triangle.1), channel_id=1, replica_groups=mesh['half'=2,'inner'=4,'loop'=4] {'half','inner','loop'}, dimensions={0} | all-to-all | bytes 1179648 | tf_op jit(solution)/shard_map/all_to_all | solution.py:334
  40.4 1.2 %update.1 = bf16[1152,128]{1,0:T(8,128)(2,1)} custom-call(bf16[2,128,1152]{2,1,0:T(8,128)(2,1)S(1)} %bitcast.8, f32[128,1152]{1,0:T(8,128)S(1)} %get-tuple-element.14.gating_ref, f32[2,128,128]{2,1,0:T(8,128)S(1)} %get-tuple-element.15.columns_ref, bf16[128,128]{1,0:T(8,128)(2,1)S(1)} %get-tuple-element.16.w_ref), custom_call_target="tpu_custom_call" | custom-call | tf_op jit(solution)/shard_map/update/pallas_call | solution.py:274

commit v9 on v8

--- a/solution.py
+++ b/solution.py
@@ -104,7 +104,7 @@
 
     @pl.loop(0, inner)
     def unpack(r):
-        blocks = [in_ref[r * loops + l].astype(jnp.float32) for l in range(loops)]
+        blocks = [in_ref[l * inner + r].astype(jnp.float32) for l in range(loops)]
         for k in range(local_rows):
             line = []
             for block in blocks:
@@ -155,7 +155,7 @@
     block = loops * local_rows + 8
     lane = lax.broadcasted_iota(jnp.int32, (inner * both, 128), 1)
 
-    blocks = [jnp.concatenate([in_ref[r * loops + l] for r in range(inner)], axis=0) for l in range(loops)]
+    blocks = [jnp.concatenate([in_ref[l * inner + r] for r in range(inner)], axis=0) for l in range(loops)]
     period = math.lcm(local_cols, 128) // local_cols
     tiles = line_tiles(local_cols)
     for u, k, count in line_groups(local_cols):
@@ -258,10 +258,13 @@
     )(*[pltpu.with_memory_space_constraint(x, pltpu.HBM) for x in given])
 
 
-def update_kernel(tri_ref, gating_ref, columns_ref, w_ref, out_ref):
+def update_kernel(inner, loops, tri_ref, gating_ref, columns_ref, w_ref, out_ref):
     values = tri_ref[0].astype(jnp.float32)
     for half in range(1, tri_ref.shape[0]):
         values += tri_ref[half].astype(jnp.float32)
+    share = values.shape[0] // (inner * loops)
+    starts = [(r * loops + l) * share for l in range(loops) for r in range(inner)]
+    values = jnp.concatenate([values[start : start + share] for start in starts], axis=0)
     center = values - jnp.mean(values, axis=0, keepdims=True)
     spread = jnp.mean(center * center, axis=0, keepdims=True)
     mixed = center * lax.rsqrt(spread + epsilon) * columns_ref[0][:, :1] + columns_ref[1][:, :1]
@@ -269,10 +272,10 @@
     out_ref[...] = (gating_ref[...] * outgoing).T.astype(jnp.bfloat16)
 
 
-def make_update(triangle, gating, columns, w_out_t):
+def make_update(inner, loops, triangle, gating, columns, w_out_t):
     channels, places = gating.shape
     return pl.pallas_call(
-        update_kernel,
+        functools.partial(update_kernel, inner, loops),
         out_shape=jax.ShapeDtypeStruct((places, channels), jnp.bfloat16),
         in_specs=[in_vmem] * 4,
         out_specs=in_vmem,
@@ -326,13 +329,13 @@
         w_out,
     )
     sides = lax.all_to_all(
-        sides.reshape(owners, 2 * share, places), ("inner", "loop"), split_axis=0, concat_axis=0
+        sides.reshape(owners, 2 * share, places), ("loop", "inner"), split_axis=0, concat_axis=0
     )
     triangle = make_triangle(
         sides, shifts, returns, halves * inner, inner, loops, local_rows, local_cols
     )
     triangle = lax.all_to_all(triangle, ("half", "inner", "loop"), split_axis=0, concat_axis=0)
-    update = make_update(triangle.reshape(halves, hidden, places), gating, columns, w_out_t)
+    update = make_update(inner, loops, triangle.reshape(halves, hidden, places), gating, columns, w_out_t)
     return update.reshape(local_rows, local_cols, channels)
 
 

time: 41.8 us -> 41.7 us (level)
  no operation moved by 1% of the time
where the time goes in v9:
time: 41.7 us; the launch traced here: 41.5 us
  blocking collectives  36.9 us (88%)
  Pallas kernels  4.56 us (11%)
    all_to_all x1, blocking collectives, on_device(): lax.all_to_all(triangle, ('half', 'inner', 'loop'), split_axis=0, concat_...  19.6 us
    all_to_all x1, blocking collectives, on_device(): lax.all_to_all(sides.reshape(owners, 2 * share, places), ('loop', 'inner'...  17.3 us
    pallas_call x1, Pallas kernels, make_sides(): pl.pallas_call(functools.partial(sides_kernel, owners, local_cols), out_s...  1.98 us
    pallas_call x1, Pallas kernels, make_triangle(): pl.pallas_call(kernel, out_shape=jax.ShapeDtypeStruct((rows * loops, shar...  1.33 us
    pallas_call x1, Pallas kernels, make_update(): pl.pallas_call(functools.partial(update_kernel, inner, loops), out_shape=...  1.24 us

profile of v9, /device:TPU:0, one launch (start us, length us, event | category | flops | bytes accessed | tf_op | source)
XLA Modules:
  0.0 41.5 jit_solution(18361956682879869564)
XLA Ops:
  0.0 2.0 %sides.1 = (bf16[256,1152]{1,0:T(8,128)(2,1)S(1)}, f32[128,1152]{1,0:T(8,128)S(1)}, f32[2,128,128]{2,1,0:T(8,128)S(1)}, bf16[128,128]{1,0:T(8,128)(2,1)S(1)}, bf...) custom-call(bf16[1152,128]{1,0:T(8,128)(2,1)} %bitcast.10, bf16[128,512]{1,0:T(8,128)(2,1)} %refs_1_.1, ...), custom_call_target="tpu_custom_call" | custom-call | tf_op jit(solution)/shard_map/sides/pallas_call | solution.py:243
  2.0 17.3 %all_to_all.10.in_ref = bf16[16,16,1152]{2,1,0:T(8,128)(2,1)S(1)} all-to-all(bf16[16,16,1152]{2,1,0:T(8,128)(2,1)S(1)} %bitcast.9), channel_id=1, replica_groups=mesh['half'=2,'inner'=4,'loop'=4] {'loop','inner'}, dimensions={0} | all-to-all | bytes 1179648 | tf_op jit(solution)/shard_map/all_to_all | solution.py:331
  19.2 1.3 %triangle.1 = bf16[32,8,1152]{2,1,0:T(8,128)(2,1)S(1)} custom-call(bf16[16,16,1152]{2,1,0:T(8,128)(2,1)S(1)} %all_to_all.10.in_ref, bf16[256,1024]{1,0:T(8,128)(2,1)S(1)} %get-tuple-element.12.shifts_ref, bf16[1280,256]{1,0:T(8,128)(2,1)S(1)} %get-tuple-element.13.returns_ref), custom_call_target="tpu_custom_call" | custom-call | tf_op jit(solution)/shard_map/triangle/pallas_call | solution.py:301
  20.6 19.6 %all_to_all.11 = bf16[32,8,1152]{2,1,0:T(8,128)(2,1)S(1)} all-to-all(bf16[32,8,1152]{2,1,0:T(8,128)(2,1)S(1)} %triangle.1), channel_id=1, replica_groups=mesh['half'=2,'inner'=4,'loop'=4] {'half','inner','loop'}, dimensions={0} | all-to-all | bytes 1179648 | tf_op jit(solution)/shard_map/all_to_all | solution.py:337
  40.2 1.2 %update.1 = bf16[1152,128]{1,0:T(8,128)(2,1)} custom-call(bf16[2,128,1152]{2,1,0:T(8,128)(2,1)S(1)} %bitcast.8, f32[128,1152]{1,0:T(8,128)S(1)} %get-tuple-element.14.gating_ref, f32[2,128,128]{2,1,0:T(8,128)S(1)} %get-tuple-element.15.columns_ref, bf16[128,128]{1,0:T(8,128)(2,1)S(1)} %get-tuple-element.16.w_ref), custom_call_target="tpu_custom_call" | custom-call | tf_op jit(solution)/shard_map/update/pallas_call | solution.py:277

commit v10 on v9

--- a/solution.py
+++ b/solution.py
@@ -269,7 +269,7 @@
     spread = jnp.mean(center * center, axis=0, keepdims=True)
     mixed = center * lax.rsqrt(spread + epsilon) * columns_ref[0][:, :1] + columns_ref[1][:, :1]
     outgoing = jnp.dot(w_ref[...], mixed.astype(jnp.bfloat16), preferred_element_type=jnp.float32)
-    out_ref[...] = (gating_ref[...] * outgoing).T.astype(jnp.bfloat16)
+    out_ref[...] = (gating_ref[...] * outgoing).astype(jnp.bfloat16).T
 
 
 def make_update(inner, loops, triangle, gating, columns, w_out_t):

time: 41.7 us -> 41.6 us (level)
  no operation moved by 1% of the time
where the time goes in v10:
time: 41.6 us; the launch traced here: 41.4 us
  blocking collectives  36.9 us (89%)
  Pallas kernels  4.53 us (11%)
    all_to_all x1, blocking collectives, on_device(): lax.all_to_all(triangle, ('half', 'inner', 'loop'), split_axis=0, concat_...  19.6 us
    all_to_all x1, blocking collectives, on_device(): lax.all_to_all(sides.reshape(owners, 2 * share, places), ('loop', 'inner'...  17.3 us
    pallas_call x1, Pallas kernels, make_sides(): pl.pallas_call(functools.partial(sides_kernel, owners, local_cols), out_s...  1.98 us
    pallas_call x1, Pallas kernels, make_triangle(): pl.pallas_call(kernel, out_shape=jax.ShapeDtypeStruct((rows * loops, shar...  1.33 us
    pallas_call x1, Pallas kernels, make_update(): pl.pallas_call(functools.partial(update_kernel, inner, loops), out_shape=...  1.21 us

profile of v10, /device:TPU:0, one launch (start us, length us, event | category | flops | bytes accessed | tf_op | source)
XLA Modules:
  0.0 41.4 jit_solution(15163677003870713311)
XLA Ops:
  0.0 2.0 %sides.1 = (bf16[256,1152]{1,0:T(8,128)(2,1)S(1)}, f32[128,1152]{1,0:T(8,128)S(1)}, f32[2,128,128]{2,1,0:T(8,128)S(1)}, bf16[128,128]{1,0:T(8,128)(2,1)S(1)}, bf...) custom-call(bf16[1152,128]{1,0:T(8,128)(2,1)} %bitcast.10, bf16[128,512]{1,0:T(8,128)(2,1)} %refs_1_.1, ...), custom_call_target="tpu_custom_call" | custom-call | tf_op jit(solution)/shard_map/sides/pallas_call | solution.py:243
  2.0 17.3 %all_to_all.10.in_ref = bf16[16,16,1152]{2,1,0:T(8,128)(2,1)S(1)} all-to-all(bf16[16,16,1152]{2,1,0:T(8,128)(2,1)S(1)} %bitcast.9), channel_id=1, replica_groups=mesh['half'=2,'inner'=4,'loop'=4] {'loop','inner'}, dimensions={0} | all-to-all | bytes 1179648 | tf_op jit(solution)/shard_map/all_to_all | solution.py:331
  19.2 1.3 %triangle.1 = bf16[32,8,1152]{2,1,0:T(8,128)(2,1)S(1)} custom-call(bf16[16,16,1152]{2,1,0:T(8,128)(2,1)S(1)} %all_to_all.10.in_ref, bf16[256,1024]{1,0:T(8,128)(2,1)S(1)} %get-tuple-element.12.shifts_ref, bf16[1280,256]{1,0:T(8,128)(2,1)S(1)} %get-tuple-element.13.returns_ref), custom_call_target="tpu_custom_call" | custom-call | tf_op jit(solution)/shard_map/triangle/pallas_call | solution.py:301
  20.6 19.6 %all_to_all.11 = bf16[32,8,1152]{2,1,0:T(8,128)(2,1)S(1)} all-to-all(bf16[32,8,1152]{2,1,0:T(8,128)(2,1)S(1)} %triangle.1), channel_id=1, replica_groups=mesh['half'=2,'inner'=4,'loop'=4] {'half','inner','loop'}, dimensions={0} | all-to-all | bytes 1179648 | tf_op jit(solution)/shard_map/all_to_all | solution.py:337
  40.2 1.2 %update.1 = bf16[1152,128]{1,0:T(8,128)(2,1)} custom-call(bf16[2,128,1152]{2,1,0:T(8,128)(2,1)S(1)} %bitcast.8, f32[128,1152]{1,0:T(8,128)S(1)} %get-tuple-element.14.gating_ref, f32[2,128,128]{2,1,0:T(8,128)S(1)} %get-tuple-element.15.columns_ref, bf16[128,128]{1,0:T(8,128)(2,1)S(1)} %get-tuple-element.16.w_ref), custom_call_target="tpu_custom_call" | custom-call | tf_op jit(solution)/shard_map/update/pallas_call | solution.py:277

commit v11 on v10

--- a/solution.py
+++ b/solution.py
@@ -80,11 +80,10 @@
     spread = jnp.mean(center * center, axis=-1, keepdims=True)
     normed = center * lax.rsqrt(spread + epsilon) * in_gain_ref[...] + in_bias_ref[...]
     normed = normed.astype(jnp.bfloat16)
-    projected, gate = [
-        lax.dot_general(weights[...], normed, (((0,), (1,)), ((), ())), preferred_element_type=jnp.float32)
-        for weights in (w_proj_ref, w_gate_ref)
-    ]
+    weights = jnp.concatenate([w_proj_ref[...], w_gate_ref[...]], axis=1)
+    projected = lax.dot_general(weights, normed, (((0,), (1,)), ((), ())), preferred_element_type=jnp.float32)
     left_gate, left, right_gate, right = [projected[n * hidden : (n + 1) * hidden] for n in range(4)]
+    gate = projected[4 * hidden :]
     left = jax.nn.sigmoid(left_gate) * left
     right = jax.nn.sigmoid(right_gate) * right
     sides = [side[at : at + share] for at in range(0, hidden, share) for side in (left, right)]

time: 41.6 us -> 41.7 us (level)
  no operation moved by 1% of the time
where the time goes in v11:
time: 41.7 us; the launch traced here: 41.5 us
  blocking collectives  36.9 us (88%)
  Pallas kernels  4.63 us (11%)
    all_to_all x1, blocking collectives, on_device(): lax.all_to_all(triangle, ('half', 'inner', 'loop'), split_axis=0, concat_...  19.6 us
    all_to_all x1, blocking collectives, on_device(): lax.all_to_all(sides.reshape(owners, 2 * share, places), ('loop', 'inner'...  17.3 us
    pallas_call x1, Pallas kernels, make_sides(): pl.pallas_call(functools.partial(sides_kernel, owners, local_cols), out_s...  2.09 us
    pallas_call x1, Pallas kernels, make_triangle(): pl.pallas_call(kernel, out_shape=jax.ShapeDtypeStruct((rows * loops, shar...  1.33 us
    pallas_call x1, Pallas kernels, make_update(): pl.pallas_call(functools.partial(update_kernel, inner, loops), out_shape=...  1.21 us

profile of v11, /device:TPU:0, one launch (start us, length us, event | category | flops | bytes accessed | tf_op | source)
XLA Modules:
  0.0 41.5 jit_solution(3614439354238067641)
XLA Ops:
  0.0 2.1 %sides.1 = (bf16[256,1152]{1,0:T(8,128)(2,1)S(1)}, f32[128,1152]{1,0:T(8,128)S(1)}, f32[2,128,128]{2,1,0:T(8,128)S(1)}, bf16[128,128]{1,0:T(8,128)(2,1)S(1)}, bf...) custom-call(bf16[1152,128]{1,0:T(8,128)(2,1)} %bitcast.10, bf16[128,512]{1,0:T(8,128)(2,1)} %refs_1_.1, ...), custom_call_target="tpu_custom_call" | custom-call | tf_op jit(solution)/shard_map/sides/pallas_call | solution.py:242
  2.1 17.3 %all_to_all.10.in_ref = bf16[16,16,1152]{2,1,0:T(8,128)(2,1)S(1)} all-to-all(bf16[16,16,1152]{2,1,0:T(8,128)(2,1)S(1)} %bitcast.9), channel_id=1, replica_groups=mesh['half'=2,'inner'=4,'loop'=4] {'loop','inner'}, dimensions={0} | all-to-all | bytes 1179648 | tf_op jit(solution)/shard_map/all_to_all | solution.py:330
  19.3 1.3 %triangle.1 = bf16[32,8,1152]{2,1,0:T(8,128)(2,1)S(1)} custom-call(bf16[16,16,1152]{2,1,0:T(8,128)(2,1)S(1)} %all_to_all.10.in_ref, bf16[256,1024]{1,0:T(8,128)(2,1)S(1)} %get-tuple-element.12.shifts_ref, bf16[1280,256]{1,0:T(8,128)(2,1)S(1)} %get-tuple-element.13.returns_ref), custom_call_target="tpu_custom_call" | custom-call | tf_op jit(solution)/shard_map/triangle/pallas_call | solution.py:300
  20.7 19.6 %all_to_all.11 = bf16[32,8,1152]{2,1,0:T(8,128)(2,1)S(1)} all-to-all(bf16[32,8,1152]{2,1,0:T(8,128)(2,1)S(1)} %triangle.1), channel_id=1, replica_groups=mesh['half'=2,'inner'=4,'loop'=4] {'half','inner','loop'}, dimensions={0} | all-to-all | bytes 1179648 | tf_op jit(solution)/shard_map/all_to_all | solution.py:336
  40.3 1.2 %update.1 = bf16[1152,128]{1,0:T(8,128)(2,1)} custom-call(bf16[2,128,1152]{2,1,0:T(8,128)(2,1)S(1)} %bitcast.8, f32[128,1152]{1,0:T(8,128)S(1)} %get-tuple-element.14.gating_ref, f32[2,128,128]{2,1,0:T(8,128)S(1)} %get-tuple-element.15.columns_ref, bf16[128,128]{1,0:T(8,128)(2,1)S(1)} %get-tuple-element.16.w_ref), custom_call_target="tpu_custom_call" | custom-call | tf_op jit(solution)/shard_map/update/pallas_call | solution.py:276

commit v12 on v10

--- a/solution.py
+++ b/solution.py
@@ -73,7 +73,12 @@
             returns_ref[begin : begin + 128, :] = jnp.where(picked, 1.0, 0.0).astype(jnp.bfloat16)
             begin += 128
 
-    for copy in copies:
+    for copy in copies[5:]:
+        copy.wait()
+    columns_ref[0] = jnp.broadcast_to(out_gain_ref[...], (128, hidden)).T
+    columns_ref[1] = jnp.broadcast_to(out_bias_ref[...], (128, hidden)).T
+    w_out_t_ref[...] = w_out_ref[...].astype(jnp.float32).T.astype(jnp.bfloat16)
+    for copy in copies[:5]:
         copy.wait()
     values = pair_ref[...].astype(jnp.float32)
     center = values - jnp.mean(values, axis=-1, keepdims=True)
@@ -90,9 +95,6 @@
     sides = [side[at : at + share] for at in range(0, hidden, share) for side in (left, right)]
     out_ref[...] = jnp.concatenate(sides, axis=0).astype(jnp.bfloat16)
     gating_ref[...] = jax.nn.sigmoid(gate)
-    columns_ref[0] = jnp.broadcast_to(out_gain_ref[...], (128, hidden)).T
-    columns_ref[1] = jnp.broadcast_to(out_bias_ref[...], (128, hidden)).T
-    w_out_t_ref[...] = w_out_ref[...].astype(jnp.float32).T.astype(jnp.bfloat16)
 
 
 def triangle_kernel(rows, inner, loops, local_rows, local_cols, pad, in_ref, out_ref, sides_ref, tri_ref):

time: 41.6 us -> 41.7 us (level)
  no operation moved by 1% of the time
where the time goes in v12:
time: 41.7 us; the launch traced here: 41.5 us
  blocking collectives  36.9 us (88%)
  Pallas kernels  4.64 us (11%)
    all_to_all x1, blocking collectives, on_device(): lax.all_to_all(triangle, ('half', 'inner', 'loop'), split_axis=0, concat_...  19.6 us
    all_to_all x1, blocking collectives, on_device(): lax.all_to_all(sides.reshape(owners, 2 * share, places), ('loop', 'inner'...  17.2 us
    pallas_call x1, Pallas kernels, make_sides(): pl.pallas_call(functools.partial(sides_kernel, owners, local_cols), out_s...  2.1 us
    pallas_call x1, Pallas kernels, make_triangle(): pl.pallas_call(kernel, out_shape=jax.ShapeDtypeStruct((rows * loops, shar...  1.33 us
    pallas_call x1, Pallas kernels, make_update(): pl.pallas_call(functools.partial(update_kernel, inner, loops), out_shape=...  1.21 us

profile of v12, /device:TPU:0, one launch (start us, length us, event | category | flops | bytes accessed | tf_op | source)
XLA Modules:
  0.0 41.5 jit_solution(13554068529326483124)
XLA Ops:
  0.0 2.1 %sides.1 = (bf16[256,1152]{1,0:T(8,128)(2,1)S(1)}, f32[128,1152]{1,0:T(8,128)S(1)}, f32[2,128,128]{2,1,0:T(8,128)S(1)}, bf16[128,128]{1,0:T(8,128)(2,1)S(1)}, bf...) custom-call(bf16[1152,128]{1,0:T(8,128)(2,1)} %bitcast.10, bf16[128,512]{1,0:T(8,128)(2,1)} %refs_1_.1, ...), custom_call_target="tpu_custom_call" | custom-call | tf_op jit(solution)/shard_map/sides/pallas_call | solution.py:245
  2.1 17.2 %all_to_all.10.in_ref = bf16[16,16,1152]{2,1,0:T(8,128)(2,1)S(1)} all-to-all(bf16[16,16,1152]{2,1,0:T(8,128)(2,1)S(1)} %bitcast.9), channel_id=1, replica_groups=mesh['half'=2,'inner'=4,'loop'=4] {'loop','inner'}, dimensions={0} | all-to-all | bytes 1179648 | tf_op jit(solution)/shard_map/all_to_all | solution.py:333
  19.4 1.3 %triangle.1 = bf16[32,8,1152]{2,1,0:T(8,128)(2,1)S(1)} custom-call(bf16[16,16,1152]{2,1,0:T(8,128)(2,1)S(1)} %all_to_all.10.in_ref, bf16[256,1024]{1,0:T(8,128)(2,1)S(1)} %get-tuple-element.12.shifts_ref, bf16[1280,256]{1,0:T(8,128)(2,1)S(1)} %get-tuple-element.13.returns_ref), custom_call_target="tpu_custom_call" | custom-call | tf_op jit(solution)/shard_map/triangle/pallas_call | solution.py:303
  20.7 19.6 %all_to_all.11 = bf16[32,8,1152]{2,1,0:T(8,128)(2,1)S(1)} all-to-all(bf16[32,8,1152]{2,1,0:T(8,128)(2,1)S(1)} %triangle.1), channel_id=1, replica_groups=mesh['half'=2,'inner'=4,'loop'=4] {'half','inner','loop'}, dimensions={0} | all-to-all | bytes 1179648 | tf_op jit(solution)/shard_map/all_to_all | solution.py:339
  40.3 1.2 %update.1 = bf16[1152,128]{1,0:T(8,128)(2,1)} custom-call(bf16[2,128,1152]{2,1,0:T(8,128)(2,1)S(1)} %bitcast.8, f32[128,1152]{1,0:T(8,128)S(1)} %get-tuple-element.14.gating_ref, f32[2,128,128]{2,1,0:T(8,128)S(1)} %get-tuple-element.15.columns_ref, bf16[128,128]{1,0:T(8,128)(2,1)S(1)} %get-tuple-element.16.w_ref), custom_call_target="tpu_custom_call" | custom-call | tf_op jit(solution)/shard_map/update/pallas_call | solution.py:279
